TPU v7x, 32 devices: a whole 2x2x4 slice. The times are simulated.
32 devices in a mesh: fsdp: 16 (over z, y, core), tensor: 2 (over x).
Axes of the slice: x: 2, y: 2, z: 4, core: 2. Of those that a mesh axis runs over, the one named last changes fastest.
Arguments:
- tokens: bfloat16 [2, 8192, 1024], P(None, ('fsdp', 'tensor')), may hold values from -6 to 6
- doc_lengths: int32 [2, 16, 4], P(None, 'fsdp'), may hold values from 1 to 256, 512 in all within a row
- attn_gain: float32 [1024], replicated, may hold values from 0.1 to 1.9
- query_weight: bfloat16 [1024, 1024], P('fsdp', 'tensor'), may hold values from -0.1875 to 0.1875
- key_weight: bfloat16 [1024, 512], P('fsdp', 'tensor'), may hold values from -0.1875 to 0.1875
- value_weight: bfloat16 [1024, 512], P('fsdp', 'tensor'), may hold values from -0.1875 to 0.1875
- query_gain: float32 [64], replicated, may hold values from 0.1 to 1.9
- key_gain: float32 [64], replicated, may hold values from 0.1 to 1.9
- out_weight: bfloat16 [1024, 1024], P('tensor', 'fsdp'), may hold values from -1 to 1
- ffn_gain: float32 [1024], replicated, may hold values from 0.1 to 1.9
- gate_weight: bfloat16 [1024, 4608], P('fsdp', 'tensor'), may hold values from -0.1875 to 0.1875
- up_weight: bfloat16 [1024, 4608], P('fsdp', 'tensor'), may hold values from -0.1875 to 0.1875
- down_weight: bfloat16 [4608, 1024], P('tensor', 'fsdp'), may hold values from -0.1875 to 0.1875
- cotangent: bfloat16 [2, 8192, 1024], P(None, ('fsdp', 'tensor')), may hold values from -6 to 6
Outputs:
- block_out: bfloat16 [2, 8192, 1024], P(None, ('fsdp', 'tensor'))
- token_grad: float32 [2, 8192, 1024], P(None, ('fsdp', 'tensor'))
- attn_gain_grad: float32 [1024], replicated
- query_weight_grad: float32 [1024, 1024], P('fsdp', 'tensor')
- key_weight_grad: float32 [1024, 512], P('fsdp', 'tensor')
- value_weight_grad: float32 [1024, 512], P('fsdp', 'tensor')
- query_gain_grad: float32 [64], replicated
- key_gain_grad: float32 [64], replicated
- out_weight_grad: float32 [1024, 1024], P('tensor', 'fsdp')
- ffn_gain_grad: float32 [1024], replicated
- gate_weight_grad: float32 [1024, 4608], P('fsdp', 'tensor')
- up_weight_grad: float32 [1024, 4608], P('fsdp', 'tensor')
- down_weight_grad: float32 [4608, 1024], P('tensor', 'fsdp')
Inputs may be any that keep to these rules, and one draw needn't show every extreme that they name: `doc_lengths`: each row of 4 document lengths sums to 512, and its longest document has exactly 256 tokens.
All inputs are finite; a program needn't handle non-finite values.
Results may differ from a plain program's by a relative error of at most 0.018.
Values may be sent and summed in bfloat16 or wider, within the bound.
A program may use at most 192 MiB of HBM per device.

v0:
```python
import math

import jax
import jax.numpy as jnp
from jax import lax
from jax.sharding import PartitionSpec as P

D = 1024
H = 16
KV = 8
HD = 64
MICRO = 2


EPSILON = 1e-05
ROPE_BASE = 1000000.0
MASKED = -1e30


def position_tables(doc_lens, row_count):
    doc_ends = jnp.cumsum(doc_lens)
    places = jnp.arange(row_count, dtype=jnp.int32)
    passed = places[:, None] >= doc_ends[None, :]
    segment = jnp.sum(passed.astype(jnp.int32), axis=-1)
    starts = jnp.sum(jnp.where(passed, doc_lens[None, :], 0), axis=-1)
    offsets = (places - starts).astype(jnp.float32)
    return (segment, offsets)


def rotary_tables(offsets, head_dim):
    half_dim = head_dim // 2
    frequency = ROPE_BASE ** (-2.0 * jnp.arange(half_dim, dtype=jnp.float32) / head_dim)
    angles = offsets[:, None] * frequency[None, :]
    return (jnp.cos(angles)[:, None, :], jnp.sin(angles)[:, None, :])


def rotary(values, cosine, sine_part):
    half_dim = values.shape[-1] // 2
    first_half = values[..., :half_dim]
    second = values[..., half_dim:]
    return jnp.concatenate(
        [first_half * cosine - second * sine_part, second * cosine + first_half * sine_part],
        axis=-1,
    )


def rotary_back(grad_in, cosine, sine_part):
    half_dim = grad_in.shape[-1] // 2
    first_half = grad_in[..., :half_dim]
    second = grad_in[..., half_dim:]
    return jnp.concatenate(
        [first_half * cosine + second * sine_part, second * cosine - first_half * sine_part],
        axis=-1,
    )


def norm_stats(values):
    return lax.rsqrt(jnp.mean(values * values, axis=-1, keepdims=True) + EPSILON)


def norm_back(values, inverse, gain_vec, grad_in):
    scaled = grad_in * gain_vec
    back_vec = inverse * scaled - values * inverse * inverse * inverse * jnp.mean(
        values * scaled, axis=-1, keepdims=True
    )
    gain_part = jnp.sum(grad_in * values * inverse, axis=tuple(range(values.ndim - 1)))
    return (back_vec, gain_part)


def masked_scores(query_b, key_b, allowed, score_scale):
    scores = (
        jnp.einsum("qngd,knd->ngqk", query_b, key_b, preferred_element_type=jnp.float32)
        * score_scale
    )
    return jnp.where(allowed[None, None], scores, MASKED)


def fetch_attention(query_weight, key_weight, value_weight, out_weight):
    return (
        lax.all_gather(query_weight, "fsdp", axis=0, tiled=True),
        lax.all_gather(key_weight, "fsdp", axis=0, tiled=True),
        lax.all_gather(value_weight, "fsdp", axis=0, tiled=True),
        lax.all_gather(out_weight, "fsdp", axis=1, tiled=True),
    )


def fetch_feed(gate_weight, up_weight, down_weight):
    return (
        lax.all_gather(gate_weight, "fsdp", axis=0, tiled=True),
        lax.all_gather(up_weight, "fsdp", axis=0, tiled=True),
        lax.all_gather(down_weight, "fsdp", axis=1, tiled=True),
    )


def gather_rows(values):
    return lax.all_gather(values, "tensor", axis=0, tiled=True)


def scatter_rows(values):
    return lax.psum_scatter(values, "tensor", scatter_dimension=0, tiled=True)


def on_device(
    tokens,
    doc_lengths,
    attn_gain,
    query_weight,
    key_weight,
    value_weight,
    query_gain,
    key_gain,
    out_weight,
    ffn_gain,
    gate_weight,
    up_weight,
    down_weight,
    cotangent,
):
    head_local = query_weight.shape[1] // HD
    kv_local = key_weight.shape[1] // HD
    group_size = H // KV
    hidden_local = gate_weight.shape[1]
    score_scale = 1.0 / math.sqrt(HD)
    local_rows = tokens.shape[1]
    seq_rows = local_rows * lax.axis_size("tensor")
    places = jnp.arange(seq_rows, dtype=jnp.int32)
    query_acc = jnp.zeros((D, head_local * HD), jnp.float32)
    key_acc = jnp.zeros((D, kv_local * HD), jnp.float32)
    value_acc = jnp.zeros((D, kv_local * HD), jnp.float32)
    out_acc = jnp.zeros((head_local * HD, D), jnp.float32)
    gate_acc = jnp.zeros((D, hidden_local), jnp.float32)
    up_acc = jnp.zeros((D, hidden_local), jnp.float32)
    down_acc = jnp.zeros((hidden_local, D), jnp.float32)
    attn_part = jnp.zeros((D,), jnp.float32)
    ffn_part = jnp.zeros((D,), jnp.float32)
    query_part = jnp.zeros((HD,), jnp.float32)
    key_part = jnp.zeros((HD,), jnp.float32)
    outputs = []
    token_grads = []
    for micro_step in range(MICRO):
        attn_set = fetch_attention(query_weight, key_weight, value_weight, out_weight)
        feed_set = fetch_feed(gate_weight, up_weight, down_weight)
        query_full, key_full, value_full, out_full = attn_set
        gate_full, up_full, down_full = feed_set
        segment, offsets = position_tables(doc_lengths[micro_step, 0], seq_rows)
        cosine, sine_part = rotary_tables(offsets, HD)
        allowed = (segment[:, None] == segment[None, :]) & (places[None, :] <= places[:, None])
        rows_in = tokens[micro_step].astype(jnp.float32)
        inverse_one = norm_stats(rows_in)
        normed_b = (rows_in * inverse_one * attn_gain).astype(jnp.bfloat16)
        gathered = gather_rows(normed_b)
        query_proj = jnp.dot(gathered, query_full, preferred_element_type=jnp.float32)
        key_proj = jnp.dot(gathered, key_full, preferred_element_type=jnp.float32)
        value_proj = jnp.dot(gathered, value_full, preferred_element_type=jnp.float32)
        query_heads = query_proj.reshape(seq_rows, head_local, HD)
        inverse_q = norm_stats(query_heads)
        query_b = rotary(query_heads * inverse_q * query_gain, cosine, sine_part).astype(
            jnp.bfloat16
        )
        query_b = query_b.reshape(seq_rows, kv_local, group_size, HD)
        key_heads = key_proj.reshape(seq_rows, kv_local, HD)
        inverse_k = norm_stats(key_heads)
        key_b = rotary(key_heads * inverse_k * key_gain, cosine, sine_part).astype(jnp.bfloat16)
        value_b = value_proj.reshape(seq_rows, kv_local, HD).astype(jnp.bfloat16)
        scores = masked_scores(query_b, key_b, allowed, score_scale)
        row_max = jnp.max(scores, axis=-1, keepdims=True)
        log_total = row_max + jnp.log(jnp.sum(jnp.exp(scores - row_max), axis=-1, keepdims=True))
        attention_b = jnp.exp(scores - log_total).astype(jnp.bfloat16)
        mixed_b = jnp.einsum(
            "ngqk,knd->qngd", attention_b, value_b, preferred_element_type=jnp.float32
        )
        mixed_b = mixed_b.reshape(seq_rows, head_local * HD).astype(jnp.bfloat16)
        attn_terms = jnp.dot(mixed_b, out_full, preferred_element_type=jnp.float32)
        hidden_one = rows_in + scatter_rows(attn_terms)
        inverse_two = norm_stats(hidden_one)
        normed_two = (hidden_one * inverse_two * ffn_gain).astype(jnp.bfloat16)
        gathered_two = gather_rows(normed_two)
        gate_act = jnp.dot(gathered_two, gate_full, preferred_element_type=jnp.float32)
        up_act = jnp.dot(gathered_two, up_full, preferred_element_type=jnp.float32)
        inner_b = (jax.nn.silu(gate_act) * up_act).astype(jnp.bfloat16)
        ffn_out = scatter_rows(jnp.dot(inner_b, down_full, preferred_element_type=jnp.float32))
        outputs.append((hidden_one + ffn_out).astype(jnp.bfloat16))
        query_full, key_full, value_full, out_full = fetch_attention(
            query_weight, key_weight, value_weight, out_weight
        )
        gate_full, up_full, down_full = fetch_feed(gate_weight, up_weight, down_weight)
        grad_out = cotangent[micro_step].astype(jnp.float32)
        grad_ffn = gather_rows(grad_out.astype(jnp.bfloat16))
        grad_inner = jnp.dot(grad_ffn, down_full.T, preferred_element_type=jnp.float32)
        down_acc = down_acc + jnp.dot(inner_b.T, grad_ffn, preferred_element_type=jnp.float32)
        sig_gate = jax.nn.sigmoid(gate_act)
        grad_gate = (grad_inner * up_act * sig_gate * (1.0 + gate_act * (1.0 - sig_gate))).astype(
            jnp.bfloat16
        )
        grad_up = (grad_inner * gate_act * sig_gate).astype(jnp.bfloat16)
        gate_acc = gate_acc + jnp.dot(gathered_two.T, grad_gate, preferred_element_type=jnp.float32)
        up_acc = up_acc + jnp.dot(gathered_two.T, grad_up, preferred_element_type=jnp.float32)
        grad_normed_two = scatter_rows(
            jnp.dot(grad_gate, gate_full.T, preferred_element_type=jnp.float32)
            + jnp.dot(grad_up, up_full.T, preferred_element_type=jnp.float32)
        )
        back_two, ffn_piece = norm_back(hidden_one, inverse_two, ffn_gain, grad_normed_two)
        ffn_part = ffn_part + ffn_piece
        grad_hidden = grad_out + back_two
        grad_attn = gather_rows(grad_hidden.astype(jnp.bfloat16))
        out_acc = out_acc + jnp.dot(mixed_b.T, grad_attn, preferred_element_type=jnp.float32)
        grad_mixed = jnp.dot(grad_attn, out_full.T, preferred_element_type=jnp.float32).astype(
            jnp.bfloat16
        )
        grad_mixed = grad_mixed.reshape(seq_rows, kv_local, group_size, HD)
        scores = masked_scores(query_b, key_b, allowed, score_scale)
        attention = jnp.exp(scores - log_total)
        attention_b = attention.astype(jnp.bfloat16)
        grad_value = jnp.einsum(
            "ngqk,qngd->knd", attention_b, grad_mixed, preferred_element_type=jnp.float32
        )
        grad_attention = jnp.einsum(
            "qngd,knd->ngqk", grad_mixed, value_b, preferred_element_type=jnp.float32
        )
        grad_scores = attention * (
            grad_attention - jnp.sum(attention * grad_attention, axis=-1, keepdims=True)
        )
        grad_scores = grad_scores.astype(jnp.bfloat16)
        grad_query = (
            jnp.einsum("ngqk,knd->qngd", grad_scores, key_b, preferred_element_type=jnp.float32)
            * score_scale
        )
        grad_key = (
            jnp.einsum("ngqk,qngd->knd", grad_scores, query_b, preferred_element_type=jnp.float32)
            * score_scale
        )
        grad_qrot = rotary_back(grad_query.reshape(seq_rows, head_local, HD), cosine, sine_part)
        back_query, query_piece = norm_back(query_heads, inverse_q, query_gain, grad_qrot)
        grad_krot = rotary_back(grad_key, cosine, sine_part)
        back_key, key_piece = norm_back(key_heads, inverse_k, key_gain, grad_krot)
        query_part = query_part + query_piece
        key_part = key_part + key_piece
        grad_query_proj = back_query.reshape(seq_rows, head_local * HD).astype(jnp.bfloat16)
        grad_key_proj = back_key.reshape(seq_rows, kv_local * HD).astype(jnp.bfloat16)
        grad_value_proj = grad_value.reshape(seq_rows, kv_local * HD).astype(jnp.bfloat16)
        query_acc = query_acc + jnp.dot(
            gathered.T, grad_query_proj, preferred_element_type=jnp.float32
        )
        key_acc = key_acc + jnp.dot(gathered.T, grad_key_proj, preferred_element_type=jnp.float32)
        value_acc = value_acc + jnp.dot(
            gathered.T, grad_value_proj, preferred_element_type=jnp.float32
        )
        grad_normed = jnp.dot(grad_query_proj, query_full.T, preferred_element_type=jnp.float32)
        grad_normed = grad_normed + jnp.dot(
            grad_key_proj, key_full.T, preferred_element_type=jnp.float32
        )
        grad_normed = grad_normed + jnp.dot(
            grad_value_proj, value_full.T, preferred_element_type=jnp.float32
        )
        grad_normed = scatter_rows(grad_normed)
        back_one, attn_piece = norm_back(rows_in, inverse_one, attn_gain, grad_normed)
        attn_part = attn_part + attn_piece
        token_grads.append(grad_hidden + back_one)
    query_grad, key_grad, value_grad, out_grad, gate_grad, up_grad, down_grad = (
        lax.psum_scatter(
            query_acc.astype(jnp.bfloat16), "fsdp", scatter_dimension=0, tiled=True
        ).astype(jnp.float32),
        lax.psum_scatter(
            key_acc.astype(jnp.bfloat16), "fsdp", scatter_dimension=0, tiled=True
        ).astype(jnp.float32),
        lax.psum_scatter(
            value_acc.astype(jnp.bfloat16), "fsdp", scatter_dimension=0, tiled=True
        ).astype(jnp.float32),
        lax.psum_scatter(
            out_acc.astype(jnp.bfloat16), "fsdp", scatter_dimension=1, tiled=True
        ).astype(jnp.float32),
        lax.psum_scatter(
            gate_acc.astype(jnp.bfloat16), "fsdp", scatter_dimension=0, tiled=True
        ).astype(jnp.float32),
        lax.psum_scatter(
            up_acc.astype(jnp.bfloat16), "fsdp", scatter_dimension=0, tiled=True
        ).astype(jnp.float32),
        lax.psum_scatter(
            down_acc.astype(jnp.bfloat16), "fsdp", scatter_dimension=1, tiled=True
        ).astype(jnp.float32),
    )
    attn_total, query_total, key_total, ffn_total = lax.psum(
        (attn_part, query_part, key_part, ffn_part), ("fsdp", "tensor")
    )
    return (
        jnp.stack(outputs),
        jnp.stack(token_grads),
        attn_total,
        query_grad,
        key_grad,
        value_grad,
        query_total,
        key_total,
        out_grad,
        ffn_total,
        gate_grad,
        up_grad,
        down_grad,
    )


def solution(mesh):
    in_specs = (
        P(None, ("fsdp", "tensor"), None),
        P(None, "fsdp", None),
        P(),
        P("fsdp", "tensor"),
        P("fsdp", "tensor"),
        P("fsdp", "tensor"),
        P(),
        P(),
        P("tensor", "fsdp"),
        P(),
        P("fsdp", "tensor"),
        P("fsdp", "tensor"),
        P("tensor", "fsdp"),
        P(None, ("fsdp", "tensor"), None),
    )
    out_specs = (
        P(None, ("fsdp", "tensor"), None),
        P(None, ("fsdp", "tensor"), None),
        P(),
        P("fsdp", "tensor"),
        P("fsdp", "tensor"),
        P("fsdp", "tensor"),
        P(),
        P(),
        P("tensor", "fsdp"),
        P(),
        P("fsdp", "tensor"),
        P("fsdp", "tensor"),
        P("tensor", "fsdp"),
    )
    return jax.shard_map(
        on_device, mesh=mesh, in_specs=in_specs, out_specs=out_specs, check_vma=False
    )
```

profile of v0, /device:TPU:0, one launch (start us, length us, event | category | flops | bytes accessed | tf_op | source)
XLA Modules:
  0.0 1306.6 jit_solution(10399492689735640464)
XLA Ops:
  9.3 2.5 fusion.28
  14.0 24.8 %all_gather.31 = bf16[1024,256]{1,0:T(8,128)(2,1)S(1)} all-gather(bf16[64,256]{1,0:T(8,128)(2,1)} %param.19), channel_id=1, replica_groups=mesh['fsdp'=16,'tensor'=2] {'fsdp'}, dimensions={0}, use_global_device_ids=true | all-gather | bytes 557056 | tf_op jit(solution)/shard_map/all_gather | solution.py:82
  39.5 18.9 %all_gather.32 = bf16[1024,256]{1,0:T(8,128)(2,1)S(1)} all-gather(bf16[64,256]{1,0:T(8,128)(2,1)S(1)} %copy-done.85), channel_id=1, replica_groups=mesh['fsdp'=16,'tensor'=2] {'fsdp'}, dimensions={0}, use_global_device_ids=true | all-gather | bytes 557056 | tf_op jit(solution)/shard_map/all_gather | solution.py:81
  59.5 2.6 multiply_reduce_fusion.13
  69.7 29.9 %all-gather.18.cloned.1.call-done = bf16[1024,512]{1,0:T(8,128)(2,1)} async-done(((bf16[64,512]{1,0:T(8,128)(2,1)}), bf16[1024,512]{1,0:T(8,128)(2,1)}) %all-gather.18.cloned.1.call-update) | async-done | bytes 1048592 | tf_op jit(solution)/shard_map/all_gather | solution.py:80
  101.7 2.4 multiply_reduce_fusion.7
  110.0 2.3 convolution_convert_fusion.1
  112.3 26.2 %all-gather.20.cloned.1.call-done = bf16[512,1024]{0,1:T(8,128)(2,1)} async-done(((bf16[512,64]{0,1:T(8,128)(2,1)}), bf16[512,1024]{0,1:T(8,128)(2,1)}) %all-gather.20.cloned.1.call-update) | async-done | bytes 1048592 | tf_op jit(solution)/shard_map/all_gather | solution.py:83
  138.5 3.3 fusion.84
  148.5 2.3 convolution_convert_fusion
  153.0 19.7 %reduce-scatter.16.cloned.1.call-done = f32[256,1024]{1,0:T(8,128)} async-done(((f32[512,1024]{1,0:T(8,128)}), f32[256,1024]{1,0:T(8,128)}) %reduce-scatter.16.cloned.1.call-update) | async-done | bytes 1048592 | tf_op jit(solution)/shard_map/reduce_scatter | solution.py:100
  172.7 34.1 %reduce-scatter.20.cloned.1.call-done = f32[256,1024]{1,0:T(8,128)} async-done(((f32[512,1024]{1,0:T(8,128)}), f32[256,1024]{1,0:T(8,128)}) %reduce-scatter.20.cloned.1.call-update) | async-done | bytes 1048592 | tf_op jit(solution)/shard_map/reduce_scatter | solution.py:100
  212.2 2.2 fusion.83
  215.6 16.5 %all-gather.22.cloned.1.call-done = bf16[512,1024]{1,0:T(8,128)(2,1)} async-done(((bf16[256,1024]{1,0:T(8,128)(2,1)}), bf16[512,1024]{1,0:T(8,128)(2,1)}) %all-gather.22.cloned.1.call-update) | async-done | bytes 1048592 | tf_op jit(solution)/shard_map/all_gather | solution.py:96
  232.1 55.7 %all-gather.24.cloned.1.call-done = bf16[1024,2304]{1,0:T(8,128)(2,1)} async-done(((bf16[64,2304]{1,0:T(8,128)(2,1)}), bf16[1024,2304]{1,0:T(8,128)(2,1)}) %all-gather.24.cloned.1.call-update) | async-done | bytes 4718608 | tf_op jit(solution)/shard_map/all_gather | solution.py:89
  287.8 7.4 fusion.85
  295.2 46.9 %all-gather.26.cloned.1.call-done = bf16[1024,2304]{1,0:T(8,128)(2,1)} async-done(((bf16[64,2304]{1,0:T(8,128)(2,1)}), bf16[1024,2304]{1,0:T(8,128)(2,1)}) %all-gather.26.cloned.1.call-update) | async-done | bytes 4718608 | tf_op jit(solution)/shard_map/all_gather | solution.py:90
  342.1 6.5 fusion.86
  348.6 15.4 %all-gather.38.cloned.1.call-done = bf16[1,512,1024]{2,1,0:T(8,128)(2,1)} async-done(((bf16[1,256,1024]{2,1,0:T(8,128)(2,1)}), bf16[1,512,1024]{2,1,0:T(8,128)(2,1)}) %all-gather.38.cloned.1.call-update) | async-done | bytes 1048592 | tf_op jit(solution)/shard_map/all_gather | solution.py:96
  363.9 55.7 %all-gather.28.cloned.1.call-done = bf16[2304,1024]{0,1:T(8,128)(2,1)} async-done(((bf16[2304,64]{0,1:T(8,128)(2,1)}), bf16[2304,1024]{0,1:T(8,128)(2,1)}) %all-gather.28.cloned.1.call-update) | async-done | bytes 4718608 | tf_op jit(solution)/shard_map/all_gather | solution.py:91
  419.6 9.4 multiply_convert_fusion.2
  429.0 6.3 fusion.92
  435.4 4.0 convolution_add_fusion.1
  439.4 30.5 %reduce-scatter.24.cloned.1.call-done = f32[256,1024]{1,0:T(8,128)} async-done(((f32[512,1024]{1,0:T(8,128)}), f32[256,1024]{1,0:T(8,128)}) %reduce-scatter.24.cloned.1.call-update) | async-done | bytes 1048592 | tf_op jit(solution)/shard_map/reduce_scatter | solution.py:100
  469.9 3.0 multiply_reduce_fusion.1
  473.7 20.7 %all-gather.32.cloned.1.call-done = bf16[512,1024]{1,0:T(8,128)(2,1)} async-done(((bf16[256,1024]{1,0:T(8,128)(2,1)}), bf16[512,1024]{1,0:T(8,128)(2,1)}) %all-gather.32.cloned.1.call-update) | async-done | bytes 1048592 | tf_op jit(solution)/shard_map/all_gather | solution.py:96
  494.3 7.5 fusion.89
  501.8 6.8 fusion.90
  508.6 8.5 all-gather.40.cloned.1.call-done
  517.1 9.4 multiply_convert_fusion
  526.5 6.2 fusion.95
  532.8 6.3 convolution_add_fusion
  539.2 7.0 fusion.87
  546.3 7.0 fusion.91
  553.4 17.8 %reduce-scatter.28.cloned.1.call-done = f32[256,1024]{1,0:T(8,128)} async-done(((f32[512,1024]{1,0:T(8,128)}), f32[256,1024]{1,0:T(8,128)}) %reduce-scatter.28.cloned.1.call-update) | async-done | bytes 1048592 | tf_op jit(solution)/shard_map/reduce_scatter | solution.py:100
  572.6 32.4 %reduce-scatter.18.cloned.1.call-done = f32[256,1024]{1,0:T(8,128)} async-done(((f32[512,1024]{1,0:T(8,128)}), f32[256,1024]{1,0:T(8,128)}) %reduce-scatter.18.cloned.1.call-update) | async-done | bytes 1048592 | tf_op jit(solution)/shard_map/reduce_scatter | solution.py:100
  605.1 34.1 %reduce-scatter.22.cloned.1.call-done = f32[256,1024]{1,0:T(8,128)} async-done(((f32[512,1024]{1,0:T(8,128)}), f32[256,1024]{1,0:T(8,128)}) %reduce-scatter.22.cloned.1.call-update) | async-done | bytes 1048592 | tf_op jit(solution)/shard_map/reduce_scatter | solution.py:100
  639.1 5.3 fusion.81
  645.5 20.4 %all-gather.34.cloned.1.call-done = bf16[512,1024]{1,0:T(8,128)(2,1)} async-done(((bf16[256,1024]{1,0:T(8,128)(2,1)}), bf16[512,1024]{1,0:T(8,128)(2,1)}) %all-gather.34.cloned.1.call-update) | async-done | bytes 1048592 | tf_op jit(solution)/shard_map/all_gather | solution.py:96
  665.9 2.3 convolution_convert_fusion.3
  668.3 5.3 fusion.3
  674.4 2.6 fusion.5
  681.1 8.3 all-gather.36.cloned.1.call-done
  691.4 5.4 fusion
  697.5 4.1 fusion.2
  705.1 3.0 fusion.20
  716.2 5.7 fusion.21
  733.7 4.5 fusion.102
  738.2 4.6 add_convert_fusion.2
  742.8 4.5 fusion.103
  747.3 4.6 add_convert_fusion.1
  753.2 4.5 fusion.53
  757.7 4.3 add_convert_fusion
  769.5 2.4 pad_maximum_fusion.1
  773.8 56.3 %reduce-scatter.36.cloned.1.call-done = bf16[64,256]{1,0:T(8,128)(2,1)} async-done(((bf16[1024,256]{1,0:T(8,128)(2,1)}), bf16[64,256]{1,0:T(8,128)(2,1)}) %reduce-scatter.36.cloned.1.call-update) | async-done | bytes 32784 | tf_op jit(solution)/shard_map/reduce_scatter | solution.py:266
  831.4 58.6 %reduce-scatter.32.cloned.1.call-done = bf16[64,512]{1,0:T(8,128)(2,1)} async-done(((bf16[1024,512]{1,0:T(8,128)(2,1)}), bf16[64,512]{1,0:T(8,128)(2,1)}) %reduce-scatter.32.cloned.1.call-update) | async-done | bytes 65552 | tf_op jit(solution)/shard_map/reduce_scatter | solution.py:260
  891.6 59.0 %reduce-scatter.38.cloned.1.call-done = bf16[512,64]{0,1:T(8,128)(2,1)} async-done(((bf16[512,1024]{0,1:T(8,128)(2,1)}), bf16[512,64]{0,1:T(8,128)(2,1)}) %reduce-scatter.38.cloned.1.call-update) | async-done | bytes 65552 | tf_op jit(solution)/shard_map/reduce_scatter | solution.py:269
  952.1 76.8 %reduce-scatter.40.cloned.1.call-done = bf16[64,2304]{1,0:T(8,128)(2,1)} async-done(((bf16[1024,2304]{1,0:T(8,128)(2,1)}), bf16[64,2304]{1,0:T(8,128)(2,1)}) %reduce-scatter.40.cloned.1.call-update) | async-done | bytes 294928 | tf_op jit(solution)/shard_map/reduce_scatter | solution.py:272
  1030.7 77.1 %reduce-scatter.42.cloned.1.call-done = bf16[64,2304]{1,0:T(8,128)(2,1)} async-done(((bf16[1024,2304]{1,0:T(8,128)(2,1)}), bf16[64,2304]{1,0:T(8,128)(2,1)}) %reduce-scatter.42.cloned.1.call-update) | async-done | bytes 294928 | tf_op jit(solution)/shard_map/reduce_scatter | solution.py:275
  1109.7 76.6 %reduce-scatter.44.cloned.1.call-done = bf16[2304,64]{0,1:T(8,128)(2,1)} async-done(((bf16[2304,1024]{0,1:T(8,128)(2,1)}), bf16[2304,64]{0,1:T(8,128)(2,1)}) %reduce-scatter.44.cloned.1.call-update) | async-done | bytes 294928 | tf_op jit(solution)/shard_map/reduce_scatter | solution.py:278
  1188.1 31.8 %reduce-scatter.26.cloned.1.call-done = f32[256,1024]{1,0:T(8,128)} async-done(((f32[512,1024]{1,0:T(8,128)}), f32[256,1024]{1,0:T(8,128)}) %reduce-scatter.26.cloned.1.call-update) | async-done | bytes 1048592 | tf_op jit(solution)/shard_map/reduce_scatter | solution.py:100
  1219.9 34.1 %reduce-scatter.30.cloned.1.call-done = f32[256,1024]{1,0:T(8,128)} async-done(((f32[512,1024]{1,0:T(8,128)}), f32[256,1024]{1,0:T(8,128)}) %reduce-scatter.30.cloned.1.call-update) | async-done | bytes 1048592 | tf_op jit(solution)/shard_map/reduce_scatter | solution.py:100
  1254.0 2.2 fusion.37
  1260.1 39.5 %all-reduce = (f32[1024]{0:T(1024)}, f32[64]{0:T(128)}, f32[64]{0:T(128)}, f32[1024]{0:T(1024)}) all-reduce(f32[1024]{0:T(1024)S(1)} %add.268, f32[64]{0:T(128)S(1)} %add.272, f32[64]{0:T(128)S(1)} %add.273, f32[1024]{0:T(1024)S(1)} %add.275), channel_id=1, replica_groups=mesh['fsdp'=16,'tensor'=2] {'fsdp','tensor'}, use_global_device_ids=true, to_apply=%region_38.39 | all-reduce | flops 2176 | bytes 17408 | tf_op jit(solution)/shard_map/psum | solution.py:282
  (394 shorter events, 94.2 us)
Async XLA Ops:
  7.2 31.6 %copy-start.95 = (s32[2,1,4]{2,1,0:T(1,128)S(1)}, s32[2,1,4]{2,1,0:T(1,128)}, u32[]{:S(2)}) copy-start(s32[2,1,4]{2,1,0:T(1,128)} %param.15) | copy-start | bytes 100
  7.2 32.3 %copy-start.85 = (bf16[64,256]{1,0:T(8,128)(2,1)S(1)}, bf16[64,256]{1,0:T(8,128)(2,1)}, u32[]{:S(2)}) copy-start(bf16[64,256]{1,0:T(8,128)(2,1)} %param.18) | copy-start | bytes 98308
  7.2 52.3 %all-gather.16.cloned.1.call-start = ((), (), s32[]{:S(2)}) async-start(), calls=%async_computation.15 | async-start | bytes 1572864 | tf_op jit(solution)/shard_map/all_gather | solution.py:96
  8.7 56.0 %copy-start.93 = (f32[64]{0:T(128)S(1)}, f32[64]{0:T(128)}, u32[]{:S(2)}) copy-start(f32[64]{0:T(128)} %param.21) | copy-start | bytes 772
  11.8 50.3 %all-gather.30.cloned.1.call-start = ((), (), s32[]{:S(2)}) async-start(), calls=%async_computation.24 | async-start | bytes 1572864 | tf_op jit(solution)/shard_map/all_gather | solution.py:96
  12.6 87.0 %all-gather.18.cloned.1.call-start = ((), (), s32[]{:S(2)}) async-start(), calls=%async_computation.16 | async-start | bytes 1114112 | tf_op jit(solution)/shard_map/all_gather | solution.py:80
  13.3 125.2 %all-gather.20.cloned.1.call-start = ((), (), s32[]{:S(2)}) async-start(), calls=%async_computation.17 | async-start | bytes 1114112 | tf_op jit(solution)/shard_map/all_gather | solution.py:83
  13.9 158.8 %reduce-scatter.16.cloned.1.call-start = ((), (), s32[]{:S(2)}) async-start(), calls=%async_computation.18 | async-start | bytes 3145728 | tf_op jit(solution)/shard_map/reduce_scatter | solution.py:100
  38.8 104.8 %copy-start.9 = (bf16[1024,256]{1,0:T(8,128)(2,1)}, bf16[1024,256]{1,0:T(8,128)(2,1)S(1)}, u32[]{:S(2)}) copy-start(bf16[1024,256]{1,0:T(8,128)(2,1)S(1)} %all_gather.31) | copy-start | bytes 1572868
  39.4 634.2 %copy-start.20 = (pred[512,512]{0,1:T(8,128)(4,1)}, pred[512,512]{0,1:T(8,128)(4,1)S(1)}, u32[]{:S(2)}) copy-start(pred[512,512]{0,1:T(8,128)(4,1)S(1)} %fusion.58) | copy-start | bytes 786436
  58.4 43.2 %copy-start.11 = (bf16[1024,256]{1,0:T(8,128)(2,1)}, bf16[1024,256]{1,0:T(8,128)(2,1)S(1)}, u32[]{:S(2)}) copy-start(bf16[1024,256]{1,0:T(8,128)(2,1)S(1)} %all_gather.32) | copy-start | bytes 1572868
  59.5 8.9 copy-start.4
  62.1 39.5 %copy-start.79 = (f32[512,4]{0,1:T(4,128)}, f32[512,4]{0,1:T(4,128)S(1)}, u32[]{:S(2)}) copy-start(f32[512,4]{0,1:T(4,128)S(1)} %add_rsqrt_fusion.3) | copy-start | bytes 24580
  63.9 37.7 %copy-start.6 = (bf16[512,1024]{1,0:T(8,128)(2,1)S(1)}, bf16[512,1024]{1,0:T(8,128)(2,1)}, u32[]{:S(2)}) copy-start(bf16[512,1024]{1,0:T(8,128)(2,1)} %all-gather.30.cloned.1.call-done) | copy-start | bytes 3145732
  64.0 40.2 %copy-start.81 = (f32[512,4]{0,1:T(4,128)}, f32[512,4]{0,1:T(4,128)S(1)}, u32[]{:S(2)}) copy-start(f32[512,4]{0,1:T(4,128)S(1)} %add_rsqrt_fusion.2) | copy-start | bytes 24580
  66.8 37.4 %copy-start.91 = (f32[64]{0:T(128)S(1)}, f32[64]{0:T(128)}, u32[]{:S(2)}) copy-start(f32[64]{0:T(128)} %param.20) | copy-start | bytes 772
  112.3 29.8 %copy-start.39 = (bf16[4,64,2,512]{3,1,2,0:T(8,128)(2,1)}, bf16[4,64,2,512]{3,1,2,0:T(8,128)(2,1)S(1)}, u32[]{:S(2)}) copy-start(bf16[4,64,2,512]{3,1,2,0:T(8,128)(2,1)S(1)} %convolution_convert_fusion.1) | copy-start | bytes 1572868
  141.8 64.9 %reduce-scatter.20.cloned.1.call-start = ((), (), s32[]{:S(2)}) async-start(), calls=%async_computation.25 | async-start | bytes 3145728 | tf_op jit(solution)/shard_map/reduce_scatter | solution.py:100
  150.8 21.9 %copy-start.41 = (bf16[4,64,2,512]{3,1,2,0:T(8,128)(2,1)}, bf16[4,64,2,512]{3,1,2,0:T(8,128)(2,1)S(1)}, u32[]{:S(2)}) copy-start(bf16[4,64,2,512]{3,1,2,0:T(8,128)(2,1)S(1)} %convolution_convert_fusion) | copy-start | bytes 1572868
  150.8 55.9 %copy-start.2 = (bf16[2,256,1024]{2,1,0:T(8,128)(2,1)S(1)}, bf16[2,256,1024]{2,1,0:T(8,128)(2,1)}, u32[]{:S(2)}) copy-start(bf16[2,256,1024]{2,1,0:T(8,128)(2,1)} %param.14) | copy-start | bytes 3145732
  150.9 58.8 %copy-start.83 = (f32[1024]{0:T(1024)S(1)}, f32[1024]{0:T(1024)}, u32[]{:S(2)}) copy-start(f32[1024]{0:T(1024)} %param.23) | copy-start | bytes 12292
  153.0 79.1 %all-gather.22.cloned.1.call-start = ((), (), s32[]{:S(2)}) async-start(), calls=%async_computation.19 | async-start | bytes 1572864 | tf_op jit(solution)/shard_map/all_gather | solution.py:96
  210.6 77.2 %all-gather.24.cloned.1.call-start = ((), (), s32[]{:S(2)}) async-start(), calls=%async_computation.20 | async-start | bytes 5013504 | tf_op jit(solution)/shard_map/all_gather | solution.py:89
  211.4 130.7 %all-gather.26.cloned.1.call-start = ((), (), s32[]{:S(2)}) async-start(), calls=%async_computation.21 | async-start | bytes 5013504 | tf_op jit(solution)/shard_map/all_gather | solution.py:90
  212.1 151.8 %all-gather.38.cloned.1.call-start = ((), (), s32[]{:S(2)}) async-start(), calls=%async_computation.41 | async-start | bytes 1572864 | tf_op jit(solution)/shard_map/all_gather | solution.py:96
  214.4 205.2 %all-gather.28.cloned.1.call-start = ((), (), s32[]{:S(2)}) async-start(), calls=%async_computation.22 | async-start | bytes 5013504 | tf_op jit(solution)/shard_map/all_gather | solution.py:91
  215.2 254.7 %reduce-scatter.24.cloned.1.call-start = ((), (), s32[]{:S(2)}) async-start(), calls=%async_computation.28 | async-start | bytes 3145728 | tf_op jit(solution)/shard_map/reduce_scatter | solution.py:100
  232.1 110.0 %copy-start.97 = (bf16[512,1024]{1,0:T(8,128)(2,1)S(1)}, bf16[512,1024]{1,0:T(8,128)(2,1)}, u32[]{:S(2)}) copy-start(bf16[512,1024]{1,0:T(8,128)(2,1)} %all-gather.22.cloned.1.call-done) | copy-start | bytes 3145732
  429.0 6.3 copy-start.104
  429.0 6.3 copy-start.103
  429.0 6.3 copy-start.96
  435.3 34.5 %copy-start.8 = (f32[256,1024]{1,0:T(8,128)S(1)}, f32[256,1024]{1,0:T(8,128)}, u32[]{:S(2)}) copy-start(f32[256,1024]{1,0:T(8,128)} %copy-done.7) | copy-start | bytes 3145732
  439.3 55.0 %all-gather.32.cloned.1.call-start = ((), (), s32[]{:S(2)}) async-start(), calls=%async_computation.26 | async-start | bytes 1572864 | tf_op jit(solution)/shard_map/all_gather | solution.py:96
  472.9 44.3 %all-gather.40.cloned.1.call-start = ((), (), s32[]{:S(2)}) async-start(), calls=%async_computation.42 | async-start | bytes 1572864 | tf_op jit(solution)/shard_map/all_gather | solution.py:96
  473.4 97.7 %reduce-scatter.28.cloned.1.call-start = ((), (), s32[]{:S(2)}) async-start(), calls=%async_computation.31 | async-start | bytes 3145728 | tf_op jit(solution)/shard_map/reduce_scatter | solution.py:100
  494.3 7.5 copy-start.101
  526.5 6.2 copy-start.108
  526.5 6.2 copy-start.106
  539.1 65.9 %reduce-scatter.18.cloned.1.call-start = ((), (), s32[]{:S(2)}) async-start(), calls=%async_computation.23 | async-start | bytes 3145728 | tf_op jit(solution)/shard_map/reduce_scatter | solution.py:100
  546.2 92.9 %reduce-scatter.22.cloned.1.call-start = ((), (), s32[]{:S(2)}) async-start(), calls=%async_computation.27 | async-start | bytes 3145728 | tf_op jit(solution)/shard_map/reduce_scatter | solution.py:100
  553.3 112.6 %all-gather.34.cloned.1.call-start = ((), (), s32[]{:S(2)}) async-start(), calls=%async_computation.29 | async-start | bytes 1572864 | tf_op jit(solution)/shard_map/all_gather | solution.py:96
  644.4 23.8 %copy-start.50 = (bf16[512,256]{0,1:T(8,128)(2,1)S(1)}, bf16[512,256]{0,1:T(8,128)(2,1)}, u32[]{:S(2)}) copy-start(bf16[512,256]{0,1:T(8,128)(2,1)} %convolution_convert_fusion.5) | copy-start | bytes 786436
  644.5 44.9 %all-gather.36.cloned.1.call-start = ((), (), s32[]{:S(2)}) async-start(), calls=%async_computation.32 | async-start | bytes 1572864 | tf_op jit(solution)/shard_map/all_gather | solution.py:96
  645.2 127.2 %reduce-scatter.34.cloned.1.call-start = ((), (), s32[]{:S(2)}) async-start(), calls=%async_computation.35 | async-start | bytes 557056 | tf_op jit(solution)/shard_map/reduce_scatter | solution.py:263
  677.1 12.3 copy-start.31
  679.3 12.1 copy-start.23
  679.3 12.1 copy-start.52
  691.4 13.6 %slice-start.4 = ((s8[8388608]{0:T(1024)(128)(4,1)}), s8[4194304]{0:T(1024)(128)(4,1)S(1)}, s32[]{:S(2)}) async-start(s8[8388608]{0:T(1024)(128)(4,1)} %bitcast.416), calls=%async_computation.47 | async-start | bytes 8388608
  697.5 7.5 slice-start.5
  714.7 115.3 %reduce-scatter.36.cloned.1.call-start = ((), (), s32[]{:S(2)}) async-start(), calls=%async_computation.36 | async-start | bytes 557056 | tf_op jit(solution)/shard_map/reduce_scatter | solution.py:266
  716.2 7.8 copy-start.78
  723.9 166.1 %reduce-scatter.32.cloned.1.call-start = ((), (), s32[]{:S(2)}) async-start(), calls=%async_computation.34 | async-start | bytes 1114112 | tf_op jit(solution)/shard_map/reduce_scatter | solution.py:260
  730.6 220.0 %reduce-scatter.38.cloned.1.call-start = ((), (), s32[]{:S(2)}) async-start(), calls=%async_computation.37 | async-start | bytes 1114112 | tf_op jit(solution)/shard_map/reduce_scatter | solution.py:269
  733.6 295.3 %reduce-scatter.40.cloned.1.call-start = ((), (), s32[]{:S(2)}) async-start(), calls=%async_computation.38 | async-start | bytes 5013504 | tf_op jit(solution)/shard_map/reduce_scatter | solution.py:272
  742.8 365.1 %reduce-scatter.42.cloned.1.call-start = ((), (), s32[]{:S(2)}) async-start(), calls=%async_computation.39 | async-start | bytes 5013504 | tf_op jit(solution)/shard_map/reduce_scatter | solution.py:275
  752.0 434.3 %reduce-scatter.44.cloned.1.call-start = ((), (), s32[]{:S(2)}) async-start(), calls=%async_computation.40 | async-start | bytes 5013504 | tf_op jit(solution)/shard_map/reduce_scatter | solution.py:278
  762.0 457.8 %reduce-scatter.26.cloned.1.call-start = ((), (), s32[]{:S(2)}) async-start(), calls=%async_computation.30 | async-start | bytes 3145728 | tf_op jit(solution)/shard_map/reduce_scatter | solution.py:100
  766.3 487.7 %reduce-scatter.30.cloned.1.call-start = ((), (), s32[]{:S(2)}) async-start(), calls=%async_computation.33 | async-start | bytes 3145728 | tf_op jit(solution)/shard_map/reduce_scatter | solution.py:100
  769.4 484.6 %copy-start.3 = (bf16[2,256,1024]{2,1,0:T(8,128)(2,1)S(1)}, bf16[2,256,1024]{2,1,0:T(8,128)(2,1)}, u32[]{:S(2)}) copy-start(bf16[2,256,1024]{2,1,0:T(8,128)(2,1)} %param.14) | copy-start | bytes 3145732
  769.4 484.6 %copy-start.84 = (f32[1024]{0:T(1024)S(1)}, f32[1024]{0:T(1024)}, u32[]{:S(2)}) copy-start(f32[1024]{0:T(1024)} %param.16) | copy-start | bytes 12292
  769.4 484.6 %copy-start.87 = (f32[256]{0:T(256)S(1)}, f32[256]{0:T(256)}, u32[]{:S(2)}) copy-start(f32[256]{0:T(256)} %copy-done.86) | copy-start | bytes 3076
  769.4 484.6 %copy-start.89 = (f32[256]{0:T(256)S(1)}, f32[256]{0:T(256)}, u32[]{:S(2)}) copy-start(f32[256]{0:T(256)} %copy-done.88) | copy-start | bytes 3076
  769.5 486.8 %copy-start.32 = (f32[256,1024]{1,0:T(8,128)S(1)}, f32[256,1024]{1,0:T(8,128)}, u32[]{:S(2)}) copy-start(f32[256,1024]{1,0:T(8,128)} %get-tuple-element.38) | copy-start | bytes 3145732
  769.5 486.8 %copy-start.33 = (f32[256,1024]{1,0:T(8,128)S(1)}, f32[256,1024]{1,0:T(8,128)}, u32[]{:S(2)}) copy-start(f32[256,1024]{1,0:T(8,128)} %get-tuple-element.70) | copy-start | bytes 3145732
  (80 other events, 221.8 us)
Sparse Core Ops, SparseCore 0:
  12.0 23.9 all-gather.15
  38.1 21.2 all-gather.29
  61.6 37.9 all-gather.17
  101.6 36.8 all-gather.19
  142.0 30.7 reduce-scatter.15
  174.9 31.8 reduce-scatter.19
  210.7 21.3 all-gather.21
  234.4 53.3 all-gather.23
  290.1 51.9 all-gather.25
  344.0 19.8 all-gather.37
  366.2 53.3 all-gather.27
  439.5 30.3 reduce-scatter.23
  473.0 21.3 all-gather.31
  495.8 21.2 all-gather.39
  539.2 31.8 reduce-scatter.27
  573.2 31.8 reduce-scatter.17
  607.2 31.8 reduce-scatter.21
  644.6 21.2 all-gather.33
  668.0 21.2 all-gather.35
  714.8 55.7 reduce-scatter.33
  775.2 54.7 reduce-scatter.35
  833.6 56.3 reduce-scatter.31
  894.1 56.4 reduce-scatter.37
  954.3 74.5 reduce-scatter.39
  1033.3 74.5 reduce-scatter.41
  1111.6 74.6 reduce-scatter.43
  1189.0 30.8 reduce-scatter.25
  1222.1 31.8 reduce-scatter.29
where the time goes:
time: 1320 us; the launch traced here: 1310 us
  waiting for transfers between devices  948 us (72%)
  matrix products  181 us (14%)
  blocking collectives  83.2 us (6%)
  other arithmetic  62.2 us (5%)
  between operations  16.5 us (1%)
    reduce_scatter x8, waiting for transfers between devices, scatter_rows(): return lax.psum_scatter(values, 'tensor', scatter_dimension=0, tiled=True)  234 us
    all_gather x8, waiting for transfers between devices, gather_rows(): return lax.all_gather(values, 'tensor', axis=0, tiled=True)  89.8 us
    reduce_scatter x1, waiting for transfers between devices, on_device(): lax.psum_scatter(up_acc.astype(jnp.bfloat16), 'fsdp', scatter_dimension=0...  77.1 us
    reduce_scatter x1, waiting for transfers between devices, on_device(): lax.psum_scatter(gate_acc.astype(jnp.bfloat16), 'fsdp', scatter_dimension...  76.8 us
    reduce_scatter x1, waiting for transfers between devices, on_device(): lax.psum_scatter(down_acc.astype(jnp.bfloat16), 'fsdp', scatter_dimension...  76.6 us
    reduce_scatter x1, waiting for transfers between devices, on_device(): lax.psum_scatter(out_acc.astype(jnp.bfloat16), 'fsdp', scatter_dimension=...  59 us
    reduce_scatter x1, waiting for transfers between devices, on_device(): lax.psum_scatter(query_acc.astype(jnp.bfloat16), 'fsdp', scatter_dimensio...  58.6 us
    reduce_scatter x1, waiting for transfers between devices, on_device(): lax.psum_scatter(value_acc.astype(jnp.bfloat16), 'fsdp', scatter_dimensio...  56.3 us
  transfers between devices with their start and end apart: 28, of which 25 were waited for; matrix products, arithmetic and copies ran while one was open for 12% of the time, Pallas kernels for 0%

commit v1 on v0

--- a/solution.py
+++ b/solution.py
@@ -299,7 +299,272 @@
     )
 
 
+def swap_tensor(values):
+    return lax.ppermute(values, "tensor", [(0, 1), (1, 0)])
+
+
+def sequence_of(values, side):
+    own = lax.dynamic_index_in_dim(values, side, 0, keepdims=False)
+    other = swap_tensor(lax.dynamic_index_in_dim(values, 1 - side, 0, keepdims=False))
+    first = jnp.where(side == 0, own, other)
+    return jnp.concatenate([first, jnp.where(side == 0, other, own)], axis=0)
+
+
+def rows_of(values, side, wire):
+    halves = values.reshape((2, values.shape[0] // 2) + values.shape[1:])
+    own = lax.dynamic_index_in_dim(halves, side, 0, keepdims=False)
+    away = lax.dynamic_index_in_dim(halves, 1 - side, 0, keepdims=False)
+    other = swap_tensor(away.astype(wire)).astype(values.dtype)
+    return jnp.stack([jnp.where(side == 0, own, other), jnp.where(side == 0, other, own)])
+
+
+def links():
+    steps, distance = [("tensor", 1)], lax.axis_size("fsdp") // 2
+    while distance:
+        steps.append(("fsdp", distance))
+        distance //= 2
+    return steps
+
+
+def exchange(values, link):
+    name, distance = link
+    pairs = [(i, i ^ distance) for i in range(lax.axis_size(name))]
+    return lax.ppermute(values, name, pairs)
+
+
+def total_of(values):
+    for link in links():
+        values = values + exchange(values, link)
+    return values
+
+
+def gather_steps(piece, order, steps):
+    for step in order:
+        other = exchange(piece, steps[step])
+        piece = jnp.concatenate([piece, other], axis=step - 1 if step else piece.ndim - 1)
+    return piece
+
+
+def scatter_steps(values, order, steps):
+    for step in order:
+        axis = step - 1 if step else values.ndim - 1
+        kept, sent = jnp.split(values, 2, axis=axis)
+        other = exchange(sent, steps[step])
+        values = (kept.astype(jnp.float32) + other.astype(jnp.float32)).astype(values.dtype)
+    return values
+
+
+def opened(weight, steps):
+    return weight.reshape((1,) * (len(steps) - 1) + weight.shape)
+
+
+def own_order(values, fsdp_index, blocks):
+    grid = values.reshape(blocks, -1)
+    return jnp.take(grid, jnp.arange(blocks) ^ fsdp_index, axis=0).reshape(values.shape)
+
+
+def times(left, right):
+    return jnp.dot(left, right, preferred_element_type=jnp.float32)
+
+
+def times_t(left, right):
+    return lax.dot_general(
+        left, right, (((1,), (1,)), ((), ())), preferred_element_type=jnp.float32
+    )
+
+
+def rows_summed(left, right):
+    return lax.dot_general(
+        left, right, (((0,), (0,)), ((), ())), preferred_element_type=jnp.float32
+    ).astype(jnp.bfloat16)
+
+
+def whole_sequence(
+    tokens,
+    doc_lengths,
+    attn_gain,
+    query_weight,
+    key_weight,
+    value_weight,
+    query_gain,
+    key_gain,
+    out_weight,
+    ffn_gain,
+    gate_weight,
+    up_weight,
+    down_weight,
+    cotangent,
+):
+    side = lax.axis_index("tensor")
+    blocks = lax.axis_size("fsdp")
+    place = lax.axis_index("fsdp")
+    q_cols = query_weight.shape[1]
+    k_cols = key_weight.shape[1]
+    group_size = H // KV
+    score_scale = 1.0 / math.sqrt(HD)
+    steps = links()
+    last = len(steps) - 1
+    far = list(range(1, last - 1))
+    orders = (
+        far + [last - 1, 0],
+        far + [0, last - 1],
+        [0, last - 1] + far,
+    )
+    qkv_local = jnp.concatenate([query_weight, key_weight, value_weight], axis=1)
+    rows_own = sequence_of(tokens, side)
+    qkv_part = gather_steps(opened(qkv_local, steps), orders[0], steps)
+    out_part = gather_steps(opened(out_weight.T, steps), orders[1], steps)
+    qkv_part, out_part, gate_local, up_local, down_local, cot_local = lax.optimization_barrier(
+        (qkv_part, out_part, gate_weight, up_weight, down_weight, cotangent)
+    )
+    qkv_full = gather_steps(qkv_part, [last], steps).reshape(D, -1)
+    out_full = gather_steps(out_part, [last], steps).reshape(D, -1)
+    cot_own = sequence_of(cot_local, side)
+    gate_full, up_full, down_full = (
+        gather_steps(opened(weight, steps), order + [last], steps).reshape(D, -1)
+        for weight, order in zip((gate_local, up_local, down_local.T), orders)
+    )
+    features = jnp.arange(D)
+    block_rows = D // blocks
+    moved = ((features // block_rows) ^ place) * block_rows + features % block_rows
+    order_mat = (moved[:, None] == features[None, :]).astype(jnp.bfloat16)
+    rows_b = times(rows_own, order_mat).astype(jnp.bfloat16)
+    cot_b = times(cot_own, order_mat).astype(jnp.bfloat16)
+    attn_gain = own_order(attn_gain, place, blocks)
+    ffn_gain = own_order(ffn_gain, place, blocks)
+    seq_rows = rows_b.shape[0]
+    lengths = lax.dynamic_index_in_dim(doc_lengths, side, 0, keepdims=False)[0]
+    segment, offsets = position_tables(lengths, seq_rows)
+    places = jnp.arange(seq_rows, dtype=jnp.int32)
+    cosine, sine_part = rotary_tables(offsets, HD)
+    allowed = (segment[:, None] == segment[None, :]) & (places[None, :] <= places[:, None])
+
+    rows_in = rows_b.astype(jnp.float32)
+    inverse_one = norm_stats(rows_in)
+    normed_b = (rows_in * inverse_one * attn_gain).astype(jnp.bfloat16)
+    v_at, one = q_cols + k_cols, q_cols + 2 * k_cols
+    projected = times(normed_b, qkv_full)
+    halves = (projected[:, :one], projected[:, one:])
+    query_proj = jnp.concatenate([p[:, :q_cols] for p in halves], axis=1)
+    key_proj = jnp.concatenate([p[:, q_cols:v_at] for p in halves], axis=1)
+    value_proj = jnp.concatenate([p[:, v_at:] for p in halves], axis=1)
+    query_heads = query_proj.reshape(seq_rows, H, HD)
+    inverse_q = norm_stats(query_heads)
+    query_b = rotary(query_heads * inverse_q * query_gain, cosine, sine_part).astype(jnp.bfloat16)
+    query_b = query_b.reshape(seq_rows, KV, group_size, HD)
+    key_heads = key_proj.reshape(seq_rows, KV, HD)
+    inverse_k = norm_stats(key_heads)
+    key_b = rotary(key_heads * inverse_k * key_gain, cosine, sine_part).astype(jnp.bfloat16)
+    value_b = value_proj.reshape(seq_rows, KV, HD).astype(jnp.bfloat16)
+    scores = masked_scores(query_b, key_b, allowed, score_scale)
+    row_max = jnp.max(scores, axis=-1, keepdims=True)
+    log_total = row_max + jnp.log(jnp.sum(jnp.exp(scores - row_max), axis=-1, keepdims=True))
+    attention = jnp.exp(scores - log_total)
+    attention_b = attention.astype(jnp.bfloat16)
+    mixed_b = jnp.einsum("ngqk,knd->qngd", attention_b, value_b, preferred_element_type=jnp.float32)
+    mixed_b = mixed_b.reshape(seq_rows, H * HD).astype(jnp.bfloat16)
+    hidden_one = rows_in + times_t(mixed_b, out_full)
+    inverse_two = norm_stats(hidden_one)
+    normed_two = (hidden_one * inverse_two * ffn_gain).astype(jnp.bfloat16)
+
+    grad_out = cot_b.astype(jnp.float32)
+    gate_act = times(normed_two, gate_full)
+    up_act = times(normed_two, up_full)
+    sig_gate = jax.nn.sigmoid(gate_act)
+    inner_b = (gate_act * sig_gate * up_act).astype(jnp.bfloat16)
+    grad_inner = times(cot_b, down_full)
+    grad_gate = (grad_inner * up_act * sig_gate * (1.0 + gate_act * (1.0 - sig_gate))).astype(
+        jnp.bfloat16
+    )
+    grad_up = (grad_inner * gate_act * sig_gate).astype(jnp.bfloat16)
+    block_out = (hidden_one + times_t(inner_b, down_full)).astype(jnp.bfloat16)
+    block_out = times(block_out, order_mat).astype(jnp.bfloat16)
+    outputs = rows_of(block_out, side, jnp.bfloat16)
+    wide = (blocks.bit_length() - 1) * (2,) + (block_rows, -1)
+
+    def scatter_grad(grad, order):
+        order = [last] + order[::-1]
+        grad = scatter_steps(grad.reshape(wide), order, steps)
+        return grad.reshape(block_rows, -1).astype(jnp.float32)
+
+    down_grad = scatter_grad(rows_summed(cot_b, inner_b), orders[2])
+    gate_grad = scatter_grad(rows_summed(normed_two, grad_gate), orders[0])
+    up_grad = scatter_grad(rows_summed(normed_two, grad_up), orders[1])
+    grad_normed_two = times_t(grad_gate, gate_full) + times_t(grad_up, up_full)
+
+    back_two, ffn_part = norm_back(hidden_one, inverse_two, ffn_gain, grad_normed_two)
+    grad_hidden = grad_out + back_two
+    grad_attn = grad_hidden.astype(jnp.bfloat16)
+    out_grad = scatter_grad(rows_summed(grad_attn, mixed_b), orders[1])
+    grad_mixed = times(grad_attn, out_full).astype(jnp.bfloat16)
+    grad_mixed = grad_mixed.reshape(seq_rows, KV, group_size, HD)
+    grad_value = jnp.einsum(
+        "ngqk,qngd->knd", attention_b, grad_mixed, preferred_element_type=jnp.float32
+    )
+    grad_attention = jnp.einsum(
+        "qngd,knd->ngqk", grad_mixed, value_b, preferred_element_type=jnp.float32
+    )
+    grad_scores = attention * (
+        grad_attention - jnp.sum(attention * grad_attention, axis=-1, keepdims=True)
+    )
+    grad_scores = grad_scores.astype(jnp.bfloat16)
+    grad_query = (
+        jnp.einsum("ngqk,knd->qngd", grad_scores, key_b, preferred_element_type=jnp.float32)
+        * score_scale
+    )
+    grad_key = (
+        jnp.einsum("ngqk,qngd->knd", grad_scores, query_b, preferred_element_type=jnp.float32)
+        * score_scale
+    )
+    grad_qrot = rotary_back(grad_query.reshape(seq_rows, H, HD), cosine, sine_part)
+    back_query, query_part = norm_back(query_heads, inverse_q, query_gain, grad_qrot)
+    grad_krot = rotary_back(grad_key, cosine, sine_part)
+    back_key, key_part = norm_back(key_heads, inverse_k, key_gain, grad_krot)
+    grad_q = back_query.reshape(seq_rows, H * HD).astype(jnp.bfloat16)
+    grad_k = back_key.reshape(seq_rows, KV * HD).astype(jnp.bfloat16)
+    grad_v = grad_value.reshape(seq_rows, KV * HD).astype(jnp.bfloat16)
+    grad_qkv = jnp.concatenate(
+        [
+            grad_q[:, :q_cols], grad_k[:, :k_cols], grad_v[:, :k_cols],
+            grad_q[:, q_cols:], grad_k[:, k_cols:], grad_v[:, k_cols:],
+        ],
+        axis=1,
+    )
+    qkv_grad = scatter_grad(rows_summed(normed_b, grad_qkv), orders[0])
+    grad_normed = times_t(grad_qkv, qkv_full)
+    back_one, attn_part = norm_back(rows_in, inverse_one, attn_gain, grad_normed)
+    token_grad = grad_hidden + back_one
+    high = token_grad.astype(jnp.bfloat16)
+    low = (token_grad - high.astype(jnp.float32)).astype(jnp.bfloat16)
+    token_grad = times(high, order_mat) + times(low, order_mat)
+    token_grad = rows_of(token_grad, side, jnp.bfloat16)
+    gain_parts = [
+        own_order(attn_part, place, blocks), own_order(ffn_part, place, blocks),
+        query_part, key_part,
+    ]
+    gain_total = total_of(jnp.concatenate(gain_parts))
+    return (
+        outputs,
+        token_grad,
+        gain_total[:D],
+        qkv_grad[:, :q_cols],
+        qkv_grad[:, q_cols:v_at],
+        qkv_grad[:, v_at:],
+        gain_total[2 * D : 2 * D + HD],
+        gain_total[2 * D + HD :],
+        out_grad.T,
+        gain_total[D : 2 * D],
+        gate_grad,
+        up_grad,
+        down_grad.T,
+    )
+
+
 def solution(mesh):
+    fsdp, tensor = mesh.shape["fsdp"], mesh.shape["tensor"]
+    run = on_device
+    if tensor == MICRO == 2 and fsdp >= 8 and fsdp & (fsdp - 1) == 0:
+        run = whole_sequence
     in_specs = (
         P(None, ("fsdp", "tensor"), None),
         P(None, "fsdp", None),
@@ -332,5 +597,5 @@
         P("tensor", "fsdp"),
     )
     return jax.shard_map(
-        on_device, mesh=mesh, in_specs=in_specs, out_specs=out_specs, check_vma=False
-    )
+        run, mesh=mesh, in_specs=in_specs, out_specs=out_specs, check_vma=False
+    )

time: 1320 us -> 698 us (0.53)
  waiting for transfers between devices: 948 us -> 279 us
  blocking collectives: 83.2 us -> 0 us
  starting transfers between devices: 2.52 us -> 73 us
  local copies, waits for them, and re-layouts: 13.2 us -> 73.7 us
  other arithmetic: 62.2 us -> 101 us
  matrix products: 181 us -> 159 us
  between operations: 16.5 us -> 3.1 us
    reduce_scatter x15 -> x0, waiting for transfers between devices: 639 us -> none  [the longest x8 234 us: scatter_rows(): return lax.psum_scatter(values, 'tensor', scatter_dimension=0, tiled=True)]
    all_gather x13 -> x0, waiting for transfers between devices: 304 us -> none  [the longest x8 89.8 us: gather_rows(): return lax.all_gather(values, 'tensor', axis=0, tiled=True)]
    ppermute x0 -> x59, waiting for transfers between devices: none -> 279 us  [the longest x55 269 us: exchange(): return lax.ppermute(values, name, pairs)]
    ppermute x0 -> x59, starting transfers between devices: none -> 73 us  [the longest x55 68.7 us: exchange(): return lax.ppermute(values, name, pairs)]
    all_gather x2 -> x0, blocking collectives: 43.7 us -> none  [the longest x1 24.8 us: fetch_attention(): lax.all_gather(value_weight, 'fsdp', axis=0, tiled=True)]
    psum x1 -> x0, blocking collectives: 39.5 us -> none  [on_device(): lax.psum((attn_part, query_part, key_part, ffn_part), ('fsdp', 'tensor'))]
    concatenate x0 -> x28, other arithmetic: none -> 33.8 us  [the longest x25 31 us: gather_steps(): jnp.concatenate([piece, other], axis=step - 1 if step else piece.ndim - 1)]
    dot_general x52 -> x24, matrix products: 178 us -> 152 us  [the longest x10 62 us: times(): return jnp.dot(left, right, preferred_element_type=jnp.float32)]
  transfers between devices with their start and end apart: 28 -> 59, of which waited for: 25 -> 31; matrix products, arithmetic and copies ran while one was open for 12% -> 24% of each run, Pallas kernels for 0% -> 0%
where the time goes in v1:
time: 698 us; the launch traced here: 689 us
  waiting for transfers between devices  279 us (40%)
  matrix products  159 us (23%)
  other arithmetic  101 us (14%)
  local copies, waits for them, and re-layouts  73.7 us (11%)
  starting transfers between devices  73 us (10%)
    ppermute x55, waiting for transfers between devices, exchange(): return lax.ppermute(values, name, pairs)  269 us
    ppermute x55, starting transfers between devices, exchange(): return lax.ppermute(values, name, pairs)  68.7 us
    dot_general x10, matrix products, times(): return jnp.dot(left, right, preferred_element_type=jnp.float32)  62 us
    dot_general x5, matrix products, rows_summed(): lax.dot_general(left, right, (((0,), (0,)), ((), ())), preferred_element_...  31.1 us
    concatenate x25, other arithmetic, gather_steps(): jnp.concatenate([piece, other], axis=step - 1 if step else piece.ndim - 1)  31 us
    dot_general x4, matrix products, times_t(): lax.dot_general(left, right, (((1,), (1,)), ((), ())), preferred_element_...  22.9 us
    convert_element_type x20, other arithmetic, scatter_steps(): (kept.astype(jnp.float32) + other.astype(jnp.float32)).astype(values.dtype)  22.6 us
    unnamed x275, local copies, waits for them, and re-layouts  15.6 us
  transfers between devices with their start and end apart: 59, of which 31 were waited for; matrix products, arithmetic and copies ran while one was open for 24% of the time, Pallas kernels for 0%

profile of v1, /device:TPU:0, one launch (start us, length us, event | category | flops | bytes accessed | tf_op | source)
XLA Modules:
  0.0 688.7 jit_solution(13833222088868966597)
XLA Ops:
  1.6 4.1 collective-permute-start.1
  15.7 5.3 collective-permute-done.2
  29.1 3.7 collective-permute-done.3
  39.9 6.7 collective-permute-done.8
  46.8 9.6 %collective-permute-done.4 = bf16[2,2,2,1,64,1024]{5,4,3,2,1,0:T(8,128)(2,1)S(1)} collective-permute-done((bf16[2,2,2,1,64,1024]{5,4,3,2,1,0:T(8,128)(2,1)S(1)}, bf16[2,2,2,1,64,1024]{5,4,3,2,1,0:T(8,128)(2,1)S(1)}, u32[]{:S(2)}, u32[]{:S(2)}) %collective-permute-start.4) | collective-permute-done | bytes 1048608 | tf_op jit(solution)/shard_map/ppermute | solution.py:332
  59.3 4.9 collective-permute-start.16
  65.3 4.9 collective-permute-start.11
  70.2 14.2 %collective-permute-done.16 = bf16[1,1,1,1,64,2304]{5,4,3,2,1,0:T(8,128)(2,1)S(1)} collective-permute-done((bf16[1,1,1,1,64,2304]{5,4,3,2,1,0:T(8,128)(2,1)S(1)}, bf16[1,1,1,1,64,2304]{5,4,3,2,1,0:T(8,128)(2,1)S(1)}, u32[]{:S(2)}, u32[]{:S(2)}) %collective-permute-start.16) | collective-permute-done | bytes 294944 | tf_op jit(solution)/shard_map/ppermute | solution.py:332
  86.0 4.1 collective-permute-done.11
  92.4 6.2 collective-permute-done.22
  98.7 26.8 %collective-permute-done.17 = bf16[2,1,1,1,64,2304]{5,4,3,2,1,0:T(8,128)(2,1)S(1)} collective-permute-done((bf16[2,1,1,1,64,2304]{5,4,3,2,1,0:T(8,128)(2,1)S(1)}, bf16[2,1,1,1,64,2304]{5,4,3,2,1,0:T(8,128)(2,1)S(1)}, u32[]{:S(2)}, u32[]{:S(2)}) %collective-permute-start.17) | collective-permute-done | bytes 589856 | tf_op jit(solution)/shard_map/ppermute | solution.py:332
  129.5 7.1 %collective-permute-done.12 = bf16[2,1,1,1,64,2304]{5,4,3,2,1,0:T(8,128)(2,1)S(1)} collective-permute-done((bf16[2,1,1,1,64,2304]{5,4,3,2,1,0:T(8,128)(2,1)S(1)}, bf16[2,1,1,1,64,2304]{5,4,3,2,1,0:T(8,128)(2,1)S(1)}, u32[]{:S(2)}, u32[]{:S(2)}) %collective-permute-start.12) | collective-permute-done | bytes 589856 | tf_op jit(solution)/shard_map/ppermute | solution.py:332
  139.8 10.9 %collective-permute-done.23 = bf16[1,1,2,1,64,4608]{5,4,3,2,1,0:T(8,128)(2,1)S(1)} collective-permute-done((bf16[1,1,2,1,64,4608]{5,4,3,2,1,0:T(8,128)(2,1)S(1)}, bf16[1,1,2,1,64,4608]{5,4,3,2,1,0:T(8,128)(2,1)S(1)}, u32[]{:S(2)}, u32[]{:S(2)}) %collective-permute-start.23) | collective-permute-done | bytes 1179680 | tf_op jit(solution)/shard_map/ppermute | solution.py:332
  156.7 8.9 %collective-permute-done.13 = bf16[2,2,1,1,64,2304]{5,4,3,2,1,0:T(8,128)(2,1)S(1)} collective-permute-done((bf16[2,2,1,1,64,2304]{5,4,3,2,1,0:T(8,128)(2,1)S(1)}, bf16[2,2,1,1,64,2304]{5,4,3,2,1,0:T(8,128)(2,1)S(1)}, u32[]{:S(2)}, u32[]{:S(2)}) %collective-permute-start.13) | collective-permute-done | bytes 1179680 | tf_op jit(solution)/shard_map/ppermute | solution.py:332
  190.1 2.9 copy.82
  200.2 2.8 collective-permute-done.24
  203.0 4.5 pad_maximum_fusion.5
  207.5 7.3 %fusion.108 = (f32[8,2,512]{2,1,0:T(2,128)S(1)}, f32[8,2,512,512]{2,3,1,0:T(8,128)}) fusion(bf16[512,8,2,32]{0,3,2,1:T(8,128)(2,1)S(1)} %bitcast.248, bf16[512,8,2,32]{0,3,2,1:T(8,128)(2,1)S(1)} %bitcast.246, bf16[512,8,32]{0,2,1:T(8,128)(2,1)S(1)} %get-tuple-element.61, bf16[512,8,32]{0,2,1:T(8,128)(2,1)S(1)} %get-tuple-element.60, ...), kind=kOutput, calls=%fused_computation.258 | convolution fusion | flops 552591360 | bytes 18644992 | tf_op jit(solution)/shard_map/qngd,knd->ngqk/dot_general | solution.py:72
  214.8 8.4 %exponential_reduce_fusion = f32[8,2,512]{2,1,0:T(2,128)S(1)} fusion(f32[8,2,512,512]{2,3,1,0:T(8,128)} %get-tuple-element.84, f32[8,2,512]{2,1,0:T(2,128)S(1)} %get-tuple-element.83), kind=kLoop, calls=%fused_computation.11 | loop fusion | flops 8380416 | bytes 16842752 | tf_op jit(solution)/shard_map/reduce_sum | solution.py:461
  226.2 8.6 %fusion.38 = bf16[8,64,2,512]{3,1,2,0:T(8,128)(2,1)S(1)} fusion(bf16[512,8,64,1]{0,2,3,1:T(8,128)(2,1)S(1)} %bitcast.235, f32[8,2,512,512]{2,3,1,0:T(8,128)} %get-tuple-element.84, f32[8,2,512]{2,1,0:T(2,128)S(1)} %bitcast.268), kind=kOutput, calls=%fused_computation.103 | convolution fusion | flops 545783808 | bytes 18382848 | tf_op jit(solution)/shard_map/ngqk,knd->qngd/dot_general | solution.py:464
  240.9 4.1 pad_maximum_fusion.2
  245.0 9.6 %fusion.110 = f32[512,4608]{1,0:T(8,128)} fusion(bf16[512,1024]{1,0:T(8,128)(2,1)} %fusion.37, bf16[1024,4608]{1,0:T(8,128)(2,1)S(1)} %bitcast.205), kind=kOutput, calls=%fused_computation.260 | convolution fusion | flops 4831838208 | bytes 19922944 | tf_op jit(solution)/shard_map/dot_general | solution.py:367
  254.6 4.2 pad_maximum_fusion.1
  258.9 7.4 %fusion.109 = f32[512,4608]{1,0:T(8,128)} fusion(bf16[512,1024]{1,0:T(8,128)(2,1)S(1)} %copy-done.72, bf16[1024,4608]{1,0:T(8,128)(2,1)S(1)} %bitcast.207), kind=kOutput, calls=%fused_computation.259 | convolution fusion | flops 4831838208 | bytes 19922944 | tf_op jit(solution)/shard_map/dot_general | solution.py:367
  266.2 5.8 pad_maximum_fusion
  272.0 18.6 %multiply_convert_fusion.1 = (bf16[512,4608]{1,0:T(8,128)(2,1)}, bf16[512,4608]{1,0:T(8,128)(2,1)}, bf16[512,4608]{1,0:T(8,128)(2,1)}) fusion(f32[512,4608]{1,0:T(8,128)} %fusion.110, f32[512,4608]{1,0:T(8,128)} %fusion.109, bf16[512,1024]{1,0:T(8,128)(2,1)} %multiply_convert_fusion.3, bf16[1024,4608]{1,0:T(8,128)(2,1)} %bitcast.209), kind=kOutput, calls=%fused_computation.23 | convolution fusion | flops 4869586944 | bytes 43515904 | tf_op jit(solution)/shard_map/dot_general | solution.py:367
  290.6 9.2 %fusion.111 = f32[512,1024]{1,0:T(8,128)S(1)} fusion(bf16[512,4608]{1,0:T(8,128)(2,1)} %get-tuple-element.38, bf16[1024,4608]{1,0:T(8,128)(2,1)} %bitcast.208), kind=kOutput, calls=%fused_computation.261 | convolution fusion | flops 4831838208 | bytes 16252928 | tf_op jit(solution)/shard_map/dot_general | solution.py:371
  299.9 5.3 multiply_reduce_fusion
  309.6 15.1 %fusion = (f32[8,2,512]{2,1,0:T(2,128)S(1)}, f32[8,512,512,2]{2,1,3,0:T(8,128)}) fusion(f32[8,2,512,512]{2,3,1,0:T(8,128)} %get-tuple-element.84, f32[8,2,512]{2,1,0:T(2,128)} %bitcast.269, bf16[512,8,64,1]{0,2,3,1:T(8,128)(2,1)S(1)} %bitcast.236, bf16[512,8,2,64]{0,3,2,1:T(8,128)(2,1)S(1)} %bitcast.203), kind=kOutput, calls=%fused_computation.6 | convolution fusion | flops 549445632 | bytes 35192832 | tf_op jit(solution)/shard_map/qngd,knd->ngqk/dot_general | solution.py:504
  324.7 8.3 %fusion.2 = bf16[8,2,512,512]{2,3,1,0:T(8,128)(2,1)S(1)} fusion(f32[8,512,512,2]{2,1,3,0:T(8,128)} %get-tuple-element.89, f32[8,2,512,512]{2,3,1,0:T(8,128)S(1)} %bitcast.192, f32[8,2,512]{2,1,0:T(2,128)S(1)} %get-tuple-element.88, f32[8,2,512]{2,1,0:T(2,128)S(1)} %bitcast.270), kind=kLoop, calls=%fused_computation.8 | loop fusion | flops 16777216 | bytes 42008576 | tf_op jit(solution)/shard_map/convert_element_type | solution.py:510
  333.1 3.3 copy-done
  336.4 2.9 convolution_multiply_fusion
  339.3 6.0 fusion.45
  345.3 3.6 fusion.46
  356.0 3.4 copy.81
  359.5 3.9 fusion.22
  376.3 6.9 %fusion.26 = (f32[1024]{0:T(1024)S(1)}, f32[512]{0:T(512)S(1)}, f32[512,1024]{1,0:T(8,128)}) fusion(bf16[512,1024]{1,0:T(8,128)(2,1)S(1)} %copy-done.113, f32[512]{0:T(512)S(1)} %copy-done.109, f32[1024]{0:T(1024)S(1)} %copy-done.103, bf16[512,2048]{1,0:T(8,128)(2,1)} %constant_dynamic-update-slice_fusion, bf16[1024,2048]{1,0:T(8,128)(2,1)} %bitcast.243), kind=kOutput, calls=%fused_computation.68 | convolution fusion | flops 2151152128 | bytes 9449472 | tf_op jit(solution)/shard_map/dot_general | solution.py:371
  383.3 4.5 convolution_convert_fusion.3
  387.8 7.6 %convolution_convert_fusion.2 = bf16[1024,4608]{1,0:T(8,128)(2,1)} fusion(bf16[512,1024]{1,0:T(8,128)(2,1)S(1)} %copy-done.73, bf16[512,4608]{1,0:T(8,128)(2,1)S(1)} %bitcast.278), kind=kOutput, calls=%fused_computation.15 | convolution fusion | flops 4836556800 | bytes 15204352 | tf_op jit(solution)/shard_map/dot_general | solution.py:377
  395.4 7.7 %convolution_convert_fusion.1 = bf16[1024,4608]{1,0:T(8,128)(2,1)} fusion(bf16[512,1024]{1,0:T(8,128)(2,1)S(1)} %copy-done.73, bf16[512,4608]{1,0:T(8,128)(2,1)S(1)} %bitcast.276), kind=kOutput, calls=%fused_computation.14 | convolution fusion | flops 4836556800 | bytes 15204352 | tf_op jit(solution)/shard_map/dot_general | solution.py:377
  403.1 12.4 %fusion.36 = bf16[512,1024]{1,0:T(8,128)(2,1)} fusion(s32[1024]{0:T(1024)S(1)} %copy-done.105, f32[512,1024]{1,0:T(8,128)S(1)} %copy-done.29, bf16[512,4608]{1,0:T(8,128)(2,1)} %get-tuple-element.37, bf16[1024,4608]{1,0:T(8,128)(2,1)} %bitcast.206), kind=kOutput, calls=%fused_computation.100 | convolution fusion | flops 5908201472 | bytes 17305600 | tf_op jit(solution)/shard_map/dot_general | solution.py:367
  415.5 10.0 %convolution_convert_fusion = bf16[1024,4608]{1,0:T(8,128)(2,1)} fusion(bf16[512,1024]{1,0:T(8,128)(2,1)S(1)} %copy-done.84, bf16[512,4608]{1,0:T(8,128)(2,1)} %get-tuple-element.37), kind=kOutput, calls=%fused_computation.13 | convolution fusion | flops 4836556800 | bytes 15204352 | tf_op jit(solution)/shard_map/dot_general | solution.py:377
  427.1 3.1 split.201
  435.5 2.8 split.221
  438.4 2.8 collective-permute-start.30
  445.2 4.4 fusion.34
  460.2 3.0 add_convert_fusion.6
  472.1 8.6 %collective-permute-done.40 = bf16[2,2,1,1,64,1024]{5,4,3,2,1,0:T(8,128)(2,1)S(1)} collective-permute-done((bf16[2,2,1,1,64,1024]{5,4,3,2,1,0:T(8,128)(2,1)S(1)}, bf16[2,2,1,1,64,1024]{5,4,3,2,1,0:T(8,128)(2,1)S(1)}, u32[]{:S(2)}, u32[]{:S(2)}) %collective-permute-start.40) | collective-permute-done | bytes 524320 | tf_op jit(solution)/shard_map/ppermute | solution.py:332
  480.9 10.8 %collective-permute-done.35 = bf16[2,2,2,1,64,1024]{5,4,3,2,1,0:T(8,128)(2,1)S(1)} collective-permute-done((bf16[2,2,2,1,64,1024]{5,4,3,2,1,0:T(8,128)(2,1)S(1)}, bf16[2,2,2,1,64,1024]{5,4,3,2,1,0:T(8,128)(2,1)S(1)}, u32[]{:S(2)}, u32[]{:S(2)}) %collective-permute-start.35) | collective-permute-done | bytes 1048608 | tf_op jit(solution)/shard_map/ppermute | solution.py:332
  492.7 10.2 %collective-permute-done.26 = bf16[256,1024]{1,0:T(8,128)(2,1)S(1)} collective-permute-done((bf16[256,1024]{1,0:T(8,128)(2,1)S(1)}, bf16[256,1024]{1,0:T(8,128)(2,1)S(1)}, u32[]{:S(2)}, u32[]{:S(2)}) %collective-permute-start.26) | collective-permute-done | bytes 524320 | tf_op jit(solution)/shard_map/ppermute | solution.py:303
  509.0 7.1 %collective-permute-done.36 = bf16[2,2,1,1,64,1024]{5,4,3,2,1,0:T(8,128)(2,1)S(1)} collective-permute-done((bf16[2,2,1,1,64,1024]{5,4,3,2,1,0:T(8,128)(2,1)S(1)}, bf16[2,2,1,1,64,1024]{5,4,3,2,1,0:T(8,128)(2,1)S(1)}, u32[]{:S(2)}, u32[]{:S(2)}) %collective-permute-start.36) | collective-permute-done | bytes 524320 | tf_op jit(solution)/shard_map/ppermute | solution.py:332
  520.3 4.1 collective-permute-done.37
  524.5 3.1 collective-permute-start.38
  528.3 2.9 collective-permute-done.38
  531.9 3.8 add_convert_fusion.2
  537.9 3.5 add_convert_fusion.1
  543.3 5.0 add_convert_fusion
  549.2 38.3 %collective-permute-done.45 = bf16[2,2,2,1,64,2304]{5,4,3,2,1,0:T(8,128)(2,1)} collective-permute-done((bf16[2,2,2,1,64,2304]{5,4,3,2,1,0:T(8,128)(2,1)}, bf16[2,2,2,1,64,2304]{5,4,3,2,1,0:T(8,128)(2,1)}, u32[]{:S(2)}, u32[]{:S(2)}) %collective-permute-start.45) | collective-permute-done | bytes 2359328 | tf_op jit(solution)/shard_map/ppermute | solution.py:332
  591.4 2.9 collective-permute-done.50
  600.4 16.1 %collective-permute-done.46 = bf16[2,2,1,1,64,2304]{5,4,3,2,1,0:T(8,128)(2,1)S(1)} collective-permute-done((bf16[2,2,1,1,64,2304]{5,4,3,2,1,0:T(8,128)(2,1)S(1)}, bf16[2,2,1,1,64,2304]{5,4,3,2,1,0:T(8,128)(2,1)S(1)}, u32[]{:S(2)}, u32[]{:S(2)}) %collective-permute-start.46) | collective-permute-done | bytes 1179680 | tf_op jit(solution)/shard_map/ppermute | solution.py:332
  619.4 28.6 %collective-permute-done.56 = bf16[1,1,2,1,64,4608]{5,4,3,2,1,0:T(8,128)(2,1)S(1)} collective-permute-done((bf16[1,1,2,1,64,4608]{5,4,3,2,1,0:T(8,128)(2,1)S(1)}, bf16[1,1,2,1,64,4608]{5,4,3,2,1,0:T(8,128)(2,1)S(1)}, u32[]{:S(2)}, u32[]{:S(2)}) %collective-permute-start.56) | collective-permute-done | bytes 1179680 | tf_op jit(solution)/shard_map/ppermute | solution.py:332
  648.8 8.9 %collective-permute-done.47 = bf16[2,1,1,1,64,2304]{5,4,3,2,1,0:T(8,128)(2,1)S(1)} collective-permute-done((bf16[2,1,1,1,64,2304]{5,4,3,2,1,0:T(8,128)(2,1)S(1)}, bf16[2,1,1,1,64,2304]{5,4,3,2,1,0:T(8,128)(2,1)S(1)}, u32[]{:S(2)}, u32[]{:S(2)}) %collective-permute-start.47) | collective-permute-done | bytes 589856 | tf_op jit(solution)/shard_map/ppermute | solution.py:332
  658.0 14.6 %collective-permute-done.52 = bf16[2,1,1,1,64,2304]{5,4,3,2,1,0:T(8,128)(2,1)S(1)} collective-permute-done((bf16[2,1,1,1,64,2304]{5,4,3,2,1,0:T(8,128)(2,1)S(1)}, bf16[2,1,1,1,64,2304]{5,4,3,2,1,0:T(8,128)(2,1)S(1)}, u32[]{:S(2)}, u32[]{:S(2)}) %collective-permute-start.52) | collective-permute-done | bytes 589856 | tf_op jit(solution)/shard_map/ppermute | solution.py:332
  675.9 10.6 %collective-permute-done.53 = bf16[1,1,1,1,64,2304]{5,4,3,2,1,0:T(8,128)(2,1)S(1)} collective-permute-done((bf16[1,1,1,1,64,2304]{5,4,3,2,1,0:T(8,128)(2,1)S(1)}, bf16[1,1,1,1,64,2304]{5,4,3,2,1,0:T(8,128)(2,1)S(1)}, u32[]{:S(2)}, u32[]{:S(2)}) %collective-permute-start.53) | collective-permute-done | bytes 294944 | tf_op jit(solution)/shard_map/ppermute | solution.py:332
  (536 shorter events, 178.7 us)
Async XLA Ops:
  1.6 12.5 %collective-permute-start.1 = (bf16[1,1,1,1,64,1024]{5,4,3,2,1,0:T(8,128)(2,1)S(1)}, bf16[1,1,1,1,64,1024]{5,4,3,2,1,0:T(8,128)(2,1)S(1)}, u32[]{:S(2)}, u32[]{:S(2)}) collective-permute-start(bf16[1,1,1,1,64,1024]{5,4,3,2,1,0:T(8,128)(2,1)S(1)} %maximum_bitcast_fusion.3), channel_id=1, source_target_pairs={{0,16},{2,18},{4,20},{6,22},{8,24},{10,26},{12,28},{14,30},{16,0},... | collective-permute-start | bytes 393224 | tf_op jit(solution)/shard_map/ppermute | solution.py:332
  5.7 16.7 %collective-permute-start.5 = (bf16[1,1,1,1,64,512]{5,4,3,2,1,0:T(8,128)(2,1)}, bf16[1,1,1,1,64,512]{5,4,3,2,1,0:T(8,128)(2,1)S(1)}, u32[]{:S(2)}, u32[]{:S(2)}) collective-permute-start(bf16[1,1,1,1,64,512]{5,4,3,2,1,0:T(8,128)(2,1)} %bitcast.261), channel_id=1, source_target_pairs={{0,16},{2,18},{4,20},{6,22},{8,24},{10,26},{12,28},{14,30},{16,0},... | collective-permute-start | bytes 196616 | tf_op jit(solution)/shard_map/ppermute | solution.py:332
  7.7 29.6 %collective-permute-start = (bf16[256,1024]{1,0:T(8,128)(2,1)}, bf16[256,1024]{1,0:T(8,128)(2,1)}, u32[]{:S(2)}, u32[]{:S(2)}) collective-permute-start(bf16[256,1024]{1,0:T(8,128)(2,1)} %dynamic-slice_bitcast_fusion.2), channel_id=1, source_target_pairs={{0,1},{1,0},{2,3},{3,2},{4,5},{5,4},{6,7},{7,6},{8,9},{9,8},{10,11... | collective-permute-start | bytes 1572872 | tf_op jit(solution)/shard_map/ppermute | solution.py:303
  14.2 6.9 collective-permute-start.2
  21.1 11.7 %collective-permute-start.3 = (bf16[2,2,1,1,64,1024]{5,4,3,2,1,0:T(8,128)(2,1)S(1)}, bf16[2,2,1,1,64,1024]{5,4,3,2,1,0:T(8,128)(2,1)S(1)}, u32[]{:S(2)}, u32[]{:S(2)}) collective-permute-start(bf16[2,2,1,1,64,1024]{5,4,3,2,1,0:T(8,128)(2,1)S(1)} %pad_maximum_fusion.29), channel_id=1, source_target_pairs={{0,4},{2,6},{4,0},{6,2},{8,12},{10,14},{12,8},{14,10},{16,20},{18,... | collective-permute-start | bytes 1572872 | tf_op jit(solution)/shard_map/ppermute | solution.py:332
  22.4 5.0 collective-permute-start.6
  24.3 145.0 %copy-start.102 = (f32[1024]{0:T(1024)}, f32[1024]{0:T(1024)S(1)}, u32[]{:S(2)}) copy-start(f32[1024]{0:T(1024)S(1)} %mul.516) | copy-start | bytes 12292
  26.3 100.8 %copy-start.104 = (s32[1024]{0:T(1024)}, s32[1024]{0:T(1024)S(1)}, u32[]{:S(2)}) copy-start(s32[1024]{0:T(1024)S(1)} %fusion.89) | copy-start | bytes 12292
  27.5 8.1 %collective-permute-start.7 = (bf16[2,2,1,1,64,512]{5,4,3,2,1,0:T(8,128)(2,1)S(1)}, bf16[2,2,1,1,64,512]{5,4,3,2,1,0:T(8,128)(2,1)S(1)}, u32[]{:S(2)}, u32[]{:S(2)}) collective-permute-start(bf16[2,2,1,1,64,512]{5,4,3,2,1,0:T(8,128)(2,1)S(1)} %pad_maximum_fusion.33), channel_id=1, source_target_pairs={{0,1},{1,0},{2,3},{3,2},{4,5},{5,4},{6,7},{7,6},{8,9},{9,8},{10,11... | collective-permute-start | bytes 786440 | tf_op jit(solution)/shard_map/ppermute | solution.py:332
  32.8 23.6 %collective-permute-start.4 = (bf16[2,2,2,1,64,1024]{5,4,3,2,1,0:T(8,128)(2,1)S(1)}, bf16[2,2,2,1,64,1024]{5,4,3,2,1,0:T(8,128)(2,1)S(1)}, u32[]{:S(2)}, u32[]{:S(2)}) collective-permute-start(bf16[2,2,2,1,64,1024]{5,4,3,2,1,0:T(8,128)(2,1)S(1)} %pad_maximum_fusion.18), channel_id=1, source_target_pairs={{0,1},{1,0},{2,3},{3,2},{4,5},{5,4},{6,7},{7,6},{8,9},{9,8},{10,11... | collective-permute-start | bytes 3145736 | tf_op jit(solution)/shard_map/ppermute | solution.py:332
  35.6 163.7 %copy-start.64 = (f32[512,32]{0,1:T(8,128)}, f32[512,32]{0,1:T(8,128)S(1)}, u32[]{:S(2)}) copy-start(f32[512,32]{0,1:T(8,128)S(1)} %get-tuple-element.71) | copy-start | bytes 196612
  35.7 11.0 %collective-permute-start.8 = (bf16[2,2,1,1,64,1024]{5,4,3,2,1,0:T(8,128)(2,1)S(1)}, bf16[2,2,1,1,64,1024]{5,4,3,2,1,0:T(8,128)(2,1)S(1)}, u32[]{:S(2)}, u32[]{:S(2)}) collective-permute-start(bf16[2,2,1,1,64,1024]{5,4,3,2,1,0:T(8,128)(2,1)S(1)} %pad_maximum_fusion.30), channel_id=1, source_target_pairs={{0,4},{2,6},{4,0},{6,2},{8,12},{10,14},{12,8},{14,10},{16,20},{18,... | collective-permute-start | bytes 1572872 | tf_op jit(solution)/shard_map/ppermute | solution.py:332
  39.9 129.4 %copy-start.111 = (bf16[512,1024]{1,0:T(8,128)(2,1)}, bf16[512,1024]{1,0:T(8,128)(2,1)S(1)}, u32[]{:S(2)}) copy-start(bf16[512,1024]{1,0:T(8,128)(2,1)S(1)} %get-tuple-element.80) | copy-start | bytes 3145732
  56.6 8.7 %collective-permute-start.21 = (bf16[1,1,1,1,64,2304]{5,4,3,2,1,0:T(8,128)(2,1)S(1)}, bf16[1,1,1,1,64,2304]{5,4,3,2,1,0:T(8,128)(2,1)S(1)}, u32[]{:S(2)}, u32[]{:S(2)}) collective-permute-start(bf16[1,1,1,1,64,2304]{5,4,3,2,1,0:T(8,128)(2,1)S(1)} %bitcast.217), channel_id=1, source_target_pairs={{0,1},{1,0},{2,3},{3,2},{4,5},{5,4},{6,7},{7,6},{8,9},{9,8},{10,11... | collective-permute-start | bytes 884744 | tf_op jit(solution)/shard_map/ppermute | solution.py:332
  58.1 111.2 %copy-start.108 = (f32[512]{0:T(512)}, f32[512]{0:T(512)S(1)}, u32[]{:S(2)}) copy-start(f32[512]{0:T(512)S(1)} %add_rsqrt_fusion.3) | copy-start | bytes 6148
  58.1 110.7 %collective-permute-start.9 = (bf16[2,2,2,1,64,2048]{5,4,3,2,1,0:T(8,128)(2,1)S(1)}, bf16[2,2,2,1,64,2048]{5,4,3,2,1,0:T(8,128)(2,1)S(1)}, u32[]{:S(2)}, u32[]{:S(2)}) collective-permute-start(bf16[2,2,2,1,64,2048]{5,4,3,2,1,0:T(8,128)(2,1)S(1)} %pad_maximum_fusion.10), channel_id=1, source_target_pairs={{0,2},{2,0},{4,6},{6,4},{8,10},{10,8},{12,14},{14,12},{16,18},{18,... | collective-permute-start | bytes 6291464 | tf_op jit(solution)/shard_map/ppermute | solution.py:332
  58.1 80.1 %collective-permute-start.10 = (bf16[2,2,2,1,64,1024]{5,4,3,2,1,0:T(8,128)(2,1)S(1)}, bf16[2,2,2,1,64,1024]{5,4,3,2,1,0:T(8,128)(2,1)S(1)}, u32[]{:S(2)}, u32[]{:S(2)}) collective-permute-start(bf16[2,2,2,1,64,1024]{5,4,3,2,1,0:T(8,128)(2,1)S(1)} %pad_maximum_fusion.19), channel_id=1, source_target_pairs={{0,2},{2,0},{4,6},{6,4},{8,10},{10,8},{12,14},{14,12},{16,18},{18,... | collective-permute-start | bytes 3145736 | tf_op jit(solution)/shard_map/ppermute | solution.py:332
  58.7 31.9 %collective-permute-start.27 = (bf16[256,1024]{1,0:T(8,128)(2,1)S(1)}, bf16[256,1024]{1,0:T(8,128)(2,1)S(1)}, u32[]{:S(2)}, u32[]{:S(2)}) collective-permute-start(bf16[256,1024]{1,0:T(8,128)(2,1)S(1)} %dynamic-slice_bitcast_fusion), channel_id=1, source_target_pairs={{0,1},{1,0},{2,3},{3,2},{4,5},{5,4},{6,7},{7,6},{8,9},{9,8},{10,11... | collective-permute-start | bytes 1572872 | tf_op jit(solution)/shard_map/ppermute | solution.py:303
  59.3 25.1 %collective-permute-start.16 = (bf16[1,1,1,1,64,2304]{5,4,3,2,1,0:T(8,128)(2,1)S(1)}, bf16[1,1,1,1,64,2304]{5,4,3,2,1,0:T(8,128)(2,1)S(1)}, u32[]{:S(2)}, u32[]{:S(2)}) collective-permute-start(bf16[1,1,1,1,64,2304]{5,4,3,2,1,0:T(8,128)(2,1)S(1)} %bitcast.223), channel_id=1, source_target_pairs={{0,16},{2,18},{4,20},{6,22},{8,24},{10,26},{12,28},{14,30},{16,0},... | collective-permute-start | bytes 884744 | tf_op jit(solution)/shard_map/ppermute | solution.py:332
  65.3 24.9 %collective-permute-start.11 = (bf16[1,1,1,1,64,2304]{5,4,3,2,1,0:T(8,128)(2,1)S(1)}, bf16[1,1,1,1,64,2304]{5,4,3,2,1,0:T(8,128)(2,1)S(1)}, u32[]{:S(2)}, u32[]{:S(2)}) collective-permute-start(bf16[1,1,1,1,64,2304]{5,4,3,2,1,0:T(8,128)(2,1)S(1)} %bitcast.229), channel_id=1, source_target_pairs={{0,16},{2,18},{4,20},{6,22},{8,24},{10,26},{12,28},{14,30},{16,0},... | collective-permute-start | bytes 884744 | tf_op jit(solution)/shard_map/ppermute | solution.py:332
  84.4 14.1 %collective-permute-start.22 = (bf16[1,1,1,1,64,4608]{5,4,3,2,1,0:T(8,128)(2,1)S(1)}, bf16[1,1,1,1,64,4608]{5,4,3,2,1,0:T(8,128)(2,1)S(1)}, u32[]{:S(2)}, u32[]{:S(2)}) collective-permute-start(bf16[1,1,1,1,64,4608]{5,4,3,2,1,0:T(8,128)(2,1)S(1)} %pad_maximum_fusion.28), channel_id=1, source_target_pairs={{0,4},{2,6},{4,0},{6,2},{8,12},{10,14},{12,8},{14,10},{16,20},{18,... | collective-permute-start | bytes 1769480 | tf_op jit(solution)/shard_map/ppermute | solution.py:332
  90.1 35.3 %collective-permute-start.17 = (bf16[2,1,1,1,64,2304]{5,4,3,2,1,0:T(8,128)(2,1)S(1)}, bf16[2,1,1,1,64,2304]{5,4,3,2,1,0:T(8,128)(2,1)S(1)}, u32[]{:S(2)}, u32[]{:S(2)}) collective-permute-start(bf16[2,1,1,1,64,2304]{5,4,3,2,1,0:T(8,128)(2,1)S(1)} %pad_maximum_fusion.27), channel_id=1, source_target_pairs={{0,8},{2,10},{4,12},{6,14},{8,0},{10,2},{12,4},{14,6},{16,24},{18,... | collective-permute-start | bytes 1769480 | tf_op jit(solution)/shard_map/ppermute | solution.py:332
  90.6 46.0 %collective-permute-start.12 = (bf16[2,1,1,1,64,2304]{5,4,3,2,1,0:T(8,128)(2,1)S(1)}, bf16[2,1,1,1,64,2304]{5,4,3,2,1,0:T(8,128)(2,1)S(1)}, u32[]{:S(2)}, u32[]{:S(2)}) collective-permute-start(bf16[2,1,1,1,64,2304]{5,4,3,2,1,0:T(8,128)(2,1)S(1)} %pad_maximum_fusion.26), channel_id=1, source_target_pairs={{0,8},{2,10},{4,12},{6,14},{8,0},{10,2},{12,4},{14,6},{16,24},{18,... | collective-permute-start | bytes 1769480 | tf_op jit(solution)/shard_map/ppermute | solution.py:332
  98.6 52.1 %collective-permute-start.23 = (bf16[1,1,2,1,64,4608]{5,4,3,2,1,0:T(8,128)(2,1)S(1)}, bf16[1,1,2,1,64,4608]{5,4,3,2,1,0:T(8,128)(2,1)S(1)}, u32[]{:S(2)}, u32[]{:S(2)}) collective-permute-start(bf16[1,1,2,1,64,4608]{5,4,3,2,1,0:T(8,128)(2,1)S(1)} %pad_maximum_fusion.17), channel_id=1, source_target_pairs={{0,16},{2,18},{4,20},{6,22},{8,24},{10,26},{12,28},{14,30},{16,0},... | collective-permute-start | bytes 3538952 | tf_op jit(solution)/shard_map/ppermute | solution.py:332
  125.6 27.8 %collective-permute-start.18 = (bf16[2,2,1,1,64,2304]{5,4,3,2,1,0:T(8,128)(2,1)S(1)}, bf16[2,2,1,1,64,2304]{5,4,3,2,1,0:T(8,128)(2,1)S(1)}, u32[]{:S(2)}, u32[]{:S(2)}) collective-permute-start(bf16[2,2,1,1,64,2304]{5,4,3,2,1,0:T(8,128)(2,1)S(1)} %pad_maximum_fusion.16), channel_id=1, source_target_pairs={{0,1},{1,0},{2,3},{3,2},{4,5},{5,4},{6,7},{7,6},{8,9},{9,8},{10,11... | collective-permute-start | bytes 3538952 | tf_op jit(solution)/shard_map/ppermute | solution.py:332
  136.7 29.0 %collective-permute-start.13 = (bf16[2,2,1,1,64,2304]{5,4,3,2,1,0:T(8,128)(2,1)S(1)}, bf16[2,2,1,1,64,2304]{5,4,3,2,1,0:T(8,128)(2,1)S(1)}, u32[]{:S(2)}, u32[]{:S(2)}) collective-permute-start(bf16[2,2,1,1,64,2304]{5,4,3,2,1,0:T(8,128)(2,1)S(1)} %pad_maximum_fusion.15), channel_id=1, source_target_pairs={{0,4},{2,6},{4,0},{6,2},{8,12},{10,14},{12,8},{14,10},{16,20},{18,... | collective-permute-start | bytes 3538952 | tf_op jit(solution)/shard_map/ppermute | solution.py:332
  152.5 50.5 %collective-permute-start.24 = (bf16[2,1,2,1,64,4608]{5,4,3,2,1,0:T(8,128)(2,1)}, bf16[2,1,2,1,64,4608]{5,4,3,2,1,0:T(8,128)(2,1)}, u32[]{:S(2)}, u32[]{:S(2)}) collective-permute-start(bf16[2,1,2,1,64,4608]{5,4,3,2,1,0:T(8,128)(2,1)} %pad_maximum_fusion.9), channel_id=1, source_target_pairs={{0,8},{2,10},{4,12},{6,14},{8,0},{10,2},{12,4},{14,6},{16,24},{18,... | collective-permute-start | bytes 7077896 | tf_op jit(solution)/shard_map/ppermute | solution.py:332
  155.2 68.1 %collective-permute-start.19 = (bf16[2,2,1,1,64,4608]{5,4,3,2,1,0:T(8,128)(2,1)}, bf16[2,2,1,1,64,4608]{5,4,3,2,1,0:T(8,128)(2,1)}, u32[]{:S(2)}, u32[]{:S(2)}) collective-permute-start(bf16[2,2,1,1,64,4608]{5,4,3,2,1,0:T(8,128)(2,1)} %pad_maximum_fusion.8), channel_id=1, source_target_pairs={{0,4},{2,6},{4,0},{6,2},{8,12},{10,14},{12,8},{14,10},{16,20},{18,... | collective-permute-start | bytes 7077896 | tf_op jit(solution)/shard_map/ppermute | solution.py:332
  167.4 71.5 %collective-permute-start.14 = (bf16[2,2,2,1,64,2304]{5,4,3,2,1,0:T(8,128)(2,1)}, bf16[2,2,2,1,64,2304]{5,4,3,2,1,0:T(8,128)(2,1)}, u32[]{:S(2)}, u32[]{:S(2)}) collective-permute-start(bf16[2,2,2,1,64,2304]{5,4,3,2,1,0:T(8,128)(2,1)} %pad_maximum_fusion.7), channel_id=1, source_target_pairs={{0,1},{1,0},{2,3},{3,2},{4,5},{5,4},{6,7},{7,6},{8,9},{9,8},{10,11... | collective-permute-start | bytes 7077896 | tf_op jit(solution)/shard_map/ppermute | solution.py:332
  207.5 33.4 %collective-permute-start.25 = (bf16[2,2,2,1,64,4608]{5,4,3,2,1,0:T(8,128)(2,1)}, bf16[2,2,2,1,64,4608]{5,4,3,2,1,0:T(8,128)(2,1)}, u32[]{:S(2)}, u32[]{:S(2)}) collective-permute-start(bf16[2,2,2,1,64,4608]{5,4,3,2,1,0:T(8,128)(2,1)} %pad_maximum_fusion.5), channel_id=1, source_target_pairs={{0,2},{2,0},{4,6},{6,4},{8,10},{10,8},{12,14},{14,12},{16,18},{18,... | collective-permute-start | bytes 14155784 | tf_op jit(solution)/shard_map/ppermute | solution.py:332
  225.7 28.9 %collective-permute-start.20 = (bf16[2,2,2,1,64,4608]{5,4,3,2,1,0:T(8,128)(2,1)S(1)}, bf16[2,2,2,1,64,4608]{5,4,3,2,1,0:T(8,128)(2,1)S(1)}, u32[]{:S(2)}, u32[]{:S(2)}) collective-permute-start(bf16[2,2,2,1,64,4608]{5,4,3,2,1,0:T(8,128)(2,1)S(1)} %pad_maximum_fusion.4), channel_id=1, source_target_pairs={{0,2},{2,0},{4,6},{6,4},{8,10},{10,8},{12,14},{14,12},{16,18},{18,... | collective-permute-start | bytes 14155784 | tf_op jit(solution)/shard_map/ppermute | solution.py:332
  240.8 25.4 %collective-permute-start.15 = (bf16[2,2,2,1,64,4608]{5,4,3,2,1,0:T(8,128)(2,1)S(1)}, bf16[2,2,2,1,64,4608]{5,4,3,2,1,0:T(8,128)(2,1)S(1)}, u32[]{:S(2)}, u32[]{:S(2)}) collective-permute-start(bf16[2,2,2,1,64,4608]{5,4,3,2,1,0:T(8,128)(2,1)S(1)} %pad_maximum_fusion.3), channel_id=1, source_target_pairs={{0,2},{2,0},{4,6},{6,4},{8,10},{10,8},{12,14},{14,12},{16,18},{18,... | collective-permute-start | bytes 14155784 | tf_op jit(solution)/shard_map/ppermute | solution.py:332
  430.3 30.0 %collective-permute-start.34 = (bf16[2,2,2,1,64,2048]{5,4,3,2,1,0:T(8,128)(2,1)}, bf16[2,2,2,1,64,2048]{5,4,3,2,1,0:T(8,128)(2,1)}, u32[]{:S(2)}, u32[]{:S(2)}) collective-permute-start(bf16[2,2,2,1,64,2048]{5,4,3,2,1,0:T(8,128)(2,1)} %split.201), channel_id=1, source_target_pairs={{0,2},{2,0},{4,6},{6,4},{8,10},{10,8},{12,14},{14,12},{16,18},{18,... | collective-permute-start | bytes 6291464 | tf_op jit(solution)/shard_map/ppermute | solution.py:332
  431.0 7.4 %collective-permute-start.29 = (f32[2176]{0:T(1024)S(1)}, f32[2176]{0:T(1024)S(1)}, u32[]{:S(2)}, u32[]{:S(2)}) collective-permute-start(f32[2176]{0:T(1024)S(1)} %concatenate.183), channel_id=1, source_target_pairs={{0,1},{1,0},{2,3},{3,2},{4,5},{5,4},{6,7},{7,6},{8,9},{9,8},{10,11... | collective-permute-start | bytes 26120 | tf_op jit(solution)/shard_map/ppermute | solution.py:332
  435.0 29.9 %collective-permute-start.39 = (bf16[2,2,2,1,64,1024]{5,4,3,2,1,0:T(8,128)(2,1)}, bf16[2,2,2,1,64,1024]{5,4,3,2,1,0:T(8,128)(2,1)}, u32[]{:S(2)}, u32[]{:S(2)}) collective-permute-start(bf16[2,2,2,1,64,1024]{5,4,3,2,1,0:T(8,128)(2,1)} %split.211), channel_id=1, source_target_pairs={{0,2},{2,0},{4,6},{6,4},{8,10},{10,8},{12,14},{14,12},{16,18},{18,... | collective-permute-start | bytes 3145736 | tf_op jit(solution)/shard_map/ppermute | solution.py:332
  438.3 93.6 %collective-permute-start.44 = (bf16[2,2,2,1,64,4608]{5,4,3,2,1,0:T(8,128)(2,1)S(1)}, bf16[2,2,2,1,64,4608]{5,4,3,2,1,0:T(8,128)(2,1)S(1)}, u32[]{:S(2)}, u32[]{:S(2)}) collective-permute-start(bf16[2,2,2,1,64,4608]{5,4,3,2,1,0:T(8,128)(2,1)S(1)} %split.221), channel_id=1, source_target_pairs={{0,2},{2,0},{4,6},{6,4},{8,10},{10,8},{12,14},{14,12},{16,18},{18,... | collective-permute-start | bytes 14155784 | tf_op jit(solution)/shard_map/ppermute | solution.py:332
  438.4 4.9 collective-permute-start.30
  443.4 6.3 collective-permute-start.31
  449.7 3.8 collective-permute-start.32
  453.4 6.6 collective-permute-start.33
  454.3 15.0 %collective-permute-start.28 = (bf16[256,1024]{1,0:T(8,128)(2,1)}, bf16[256,1024]{1,0:T(8,128)(2,1)}, u32[]{:S(2)}, u32[]{:S(2)}) collective-permute-start(bf16[256,1024]{1,0:T(8,128)(2,1)} %fusion.63), channel_id=1, source_target_pairs={{0,1},{1,0},{2,3},{3,2},{4,5},{5,4},{6,7},{7,6},{8,9},{9,8},{10,11... | collective-permute-start | bytes 1572872 | tf_op jit(solution)/shard_map/ppermute | solution.py:303
  460.0 77.9 %collective-permute-start.49 = (bf16[2,2,2,1,64,4608]{5,4,3,2,1,0:T(8,128)(2,1)}, bf16[2,2,2,1,64,4608]{5,4,3,2,1,0:T(8,128)(2,1)}, u32[]{:S(2)}, u32[]{:S(2)}) collective-permute-start(bf16[2,2,2,1,64,4608]{5,4,3,2,1,0:T(8,128)(2,1)} %split.231), channel_id=1, source_target_pairs={{0,2},{2,0},{4,6},{6,4},{8,10},{10,8},{12,14},{14,12},{16,18},{18,... | collective-permute-start | bytes 14155784 | tf_op jit(solution)/shard_map/ppermute | solution.py:332
  463.4 28.4 %collective-permute-start.35 = (bf16[2,2,2,1,64,1024]{5,4,3,2,1,0:T(8,128)(2,1)S(1)}, bf16[2,2,2,1,64,1024]{5,4,3,2,1,0:T(8,128)(2,1)S(1)}, u32[]{:S(2)}, u32[]{:S(2)}) collective-permute-start(bf16[2,2,2,1,64,1024]{5,4,3,2,1,0:T(8,128)(2,1)S(1)} %split.203), channel_id=1, source_target_pairs={{0,1},{1,0},{2,3},{3,2},{4,5},{5,4},{6,7},{7,6},{8,9},{9,8},{10,11... | collective-permute-start | bytes 3145736 | tf_op jit(solution)/shard_map/ppermute | solution.py:332
  466.6 14.1 %collective-permute-start.40 = (bf16[2,2,1,1,64,1024]{5,4,3,2,1,0:T(8,128)(2,1)S(1)}, bf16[2,2,1,1,64,1024]{5,4,3,2,1,0:T(8,128)(2,1)S(1)}, u32[]{:S(2)}, u32[]{:S(2)}) collective-permute-start(bf16[2,2,1,1,64,1024]{5,4,3,2,1,0:T(8,128)(2,1)S(1)} %split.213), channel_id=1, source_target_pairs={{0,4},{2,6},{4,0},{6,2},{8,12},{10,14},{12,8},{14,10},{16,20},{18,... | collective-permute-start | bytes 1572872 | tf_op jit(solution)/shard_map/ppermute | solution.py:332
  469.4 33.6 %collective-permute-start.26 = (bf16[256,1024]{1,0:T(8,128)(2,1)S(1)}, bf16[256,1024]{1,0:T(8,128)(2,1)S(1)}, u32[]{:S(2)}, u32[]{:S(2)}) collective-permute-start(bf16[256,1024]{1,0:T(8,128)(2,1)S(1)} %dynamic-slice_bitcast_fusion.1), channel_id=1, source_target_pairs={{0,1},{1,0},{2,3},{3,2},{4,5},{5,4},{6,7},{7,6},{8,9},{9,8},{10,11... | collective-permute-start | bytes 1572872 | tf_op jit(solution)/shard_map/ppermute | solution.py:303
  480.7 62.6 %collective-permute-start.54 = (bf16[2,2,2,1,64,4608]{5,4,3,2,1,0:T(8,128)(2,1)}, bf16[2,2,2,1,64,4608]{5,4,3,2,1,0:T(8,128)(2,1)}, u32[]{:S(2)}, u32[]{:S(2)}) collective-permute-start(bf16[2,2,2,1,64,4608]{5,4,3,2,1,0:T(8,128)(2,1)} %split.241), channel_id=1, source_target_pairs={{0,2},{2,0},{4,6},{6,4},{8,10},{10,8},{12,14},{14,12},{16,18},{18,... | collective-permute-start | bytes 14155784 | tf_op jit(solution)/shard_map/ppermute | solution.py:332
  491.7 16.5 %collective-permute-start.41 = (bf16[2,2,1,1,64,512]{5,4,3,2,1,0:T(8,128)(2,1)S(1)}, bf16[2,2,1,1,64,512]{5,4,3,2,1,0:T(8,128)(2,1)S(1)}, u32[]{:S(2)}, u32[]{:S(2)}) collective-permute-start(bf16[2,2,1,1,64,512]{5,4,3,2,1,0:T(8,128)(2,1)S(1)} %split.215), channel_id=1, source_target_pairs={{0,1},{1,0},{2,3},{3,2},{4,5},{5,4},{6,7},{7,6},{8,9},{9,8},{10,11... | collective-permute-start | bytes 786440 | tf_op jit(solution)/shard_map/ppermute | solution.py:332
  503.0 13.1 %collective-permute-start.36 = (bf16[2,2,1,1,64,1024]{5,4,3,2,1,0:T(8,128)(2,1)S(1)}, bf16[2,2,1,1,64,1024]{5,4,3,2,1,0:T(8,128)(2,1)S(1)}, u32[]{:S(2)}, u32[]{:S(2)}) collective-permute-start(bf16[2,2,1,1,64,1024]{5,4,3,2,1,0:T(8,128)(2,1)S(1)} %split.205), channel_id=1, source_target_pairs={{0,4},{2,6},{4,0},{6,2},{8,12},{10,14},{12,8},{14,10},{16,20},{18,... | collective-permute-start | bytes 1572872 | tf_op jit(solution)/shard_map/ppermute | solution.py:332
  508.3 9.8 %collective-permute-start.42 = (bf16[2,1,1,1,64,512]{5,4,3,2,1,0:T(8,128)(2,1)S(1)}, bf16[2,1,1,1,64,512]{5,4,3,2,1,0:T(8,128)(2,1)S(1)}, u32[]{:S(2)}, u32[]{:S(2)}) collective-permute-start(bf16[2,1,1,1,64,512]{5,4,3,2,1,0:T(8,128)(2,1)S(1)} %split.217), channel_id=1, source_target_pairs={{0,8},{2,10},{4,12},{6,14},{8,0},{10,2},{12,4},{14,6},{16,24},{18,... | collective-permute-start | bytes 393224 | tf_op jit(solution)/shard_map/ppermute | solution.py:332
  516.3 8.1 %collective-permute-start.37 = (bf16[2,1,1,1,64,1024]{5,4,3,2,1,0:T(8,128)(2,1)S(1)}, bf16[2,1,1,1,64,1024]{5,4,3,2,1,0:T(8,128)(2,1)S(1)}, u32[]{:S(2)}, u32[]{:S(2)}) collective-permute-start(bf16[2,1,1,1,64,1024]{5,4,3,2,1,0:T(8,128)(2,1)S(1)} %split.207), channel_id=1, source_target_pairs={{0,8},{2,10},{4,12},{6,14},{8,0},{10,2},{12,4},{14,6},{16,24},{18,... | collective-permute-start | bytes 786440 | tf_op jit(solution)/shard_map/ppermute | solution.py:332
  518.2 9.4 %collective-permute-start.43 = (bf16[1,1,1,1,64,512]{5,4,3,2,1,0:T(8,128)(2,1)S(1)}, bf16[1,1,1,1,64,512]{5,4,3,2,1,0:T(8,128)(2,1)S(1)}, u32[]{:S(2)}, u32[]{:S(2)}) collective-permute-start(bf16[1,1,1,1,64,512]{5,4,3,2,1,0:T(8,128)(2,1)S(1)} %split.219), channel_id=1, source_target_pairs={{0,16},{2,18},{4,20},{6,22},{8,24},{10,26},{12,28},{14,30},{16,0},... | collective-permute-start | bytes 196616 | tf_op jit(solution)/shard_map/ppermute | solution.py:332
  524.5 6.7 collective-permute-start.38
  537.4 50.1 %collective-permute-start.45 = (bf16[2,2,2,1,64,2304]{5,4,3,2,1,0:T(8,128)(2,1)}, bf16[2,2,2,1,64,2304]{5,4,3,2,1,0:T(8,128)(2,1)}, u32[]{:S(2)}, u32[]{:S(2)}) collective-permute-start(bf16[2,2,2,1,64,2304]{5,4,3,2,1,0:T(8,128)(2,1)} %split.223), channel_id=1, source_target_pairs={{0,1},{1,0},{2,3},{3,2},{4,5},{5,4},{6,7},{7,6},{8,9},{9,8},{10,11... | collective-permute-start | bytes 7077896 | tf_op jit(solution)/shard_map/ppermute | solution.py:332
  541.7 52.6 %collective-permute-start.50 = (bf16[2,2,1,1,64,4608]{5,4,3,2,1,0:T(8,128)(2,1)S(1)}, bf16[2,2,1,1,64,4608]{5,4,3,2,1,0:T(8,128)(2,1)S(1)}, u32[]{:S(2)}, u32[]{:S(2)}) collective-permute-start(bf16[2,2,1,1,64,4608]{5,4,3,2,1,0:T(8,128)(2,1)S(1)} %split.233), channel_id=1, source_target_pairs={{0,4},{2,6},{4,0},{6,2},{8,12},{10,14},{12,8},{14,10},{16,20},{18,... | collective-permute-start | bytes 7077896 | tf_op jit(solution)/shard_map/ppermute | solution.py:332
  548.4 49.9 %collective-permute-start.55 = (bf16[2,1,2,1,64,4608]{5,4,3,2,1,0:T(8,128)(2,1)S(1)}, bf16[2,1,2,1,64,4608]{5,4,3,2,1,0:T(8,128)(2,1)S(1)}, u32[]{:S(2)}, u32[]{:S(2)}) collective-permute-start(bf16[2,1,2,1,64,4608]{5,4,3,2,1,0:T(8,128)(2,1)S(1)} %split.243), channel_id=1, source_target_pairs={{0,8},{2,10},{4,12},{6,14},{8,0},{10,2},{12,4},{14,6},{16,24},{18,... | collective-permute-start | bytes 7077896 | tf_op jit(solution)/shard_map/ppermute | solution.py:332
  589.8 26.7 %collective-permute-start.46 = (bf16[2,2,1,1,64,2304]{5,4,3,2,1,0:T(8,128)(2,1)S(1)}, bf16[2,2,1,1,64,2304]{5,4,3,2,1,0:T(8,128)(2,1)S(1)}, u32[]{:S(2)}, u32[]{:S(2)}) collective-permute-start(bf16[2,2,1,1,64,2304]{5,4,3,2,1,0:T(8,128)(2,1)S(1)} %split.225), channel_id=1, source_target_pairs={{0,4},{2,6},{4,0},{6,2},{8,12},{10,14},{12,8},{14,10},{16,20},{18,... | collective-permute-start | bytes 3538952 | tf_op jit(solution)/shard_map/ppermute | solution.py:332
  594.9 22.0 %collective-permute-start.51 = (bf16[2,2,1,1,64,2304]{5,4,3,2,1,0:T(8,128)(2,1)S(1)}, bf16[2,2,1,1,64,2304]{5,4,3,2,1,0:T(8,128)(2,1)S(1)}, u32[]{:S(2)}, u32[]{:S(2)}) collective-permute-start(bf16[2,2,1,1,64,2304]{5,4,3,2,1,0:T(8,128)(2,1)S(1)} %split.235), channel_id=1, source_target_pairs={{0,1},{1,0},{2,3},{3,2},{4,5},{5,4},{6,7},{7,6},{8,9},{9,8},{10,11... | collective-permute-start | bytes 3538952 | tf_op jit(solution)/shard_map/ppermute | solution.py:332
  599.1 48.9 %collective-permute-start.56 = (bf16[1,1,2,1,64,4608]{5,4,3,2,1,0:T(8,128)(2,1)S(1)}, bf16[1,1,2,1,64,4608]{5,4,3,2,1,0:T(8,128)(2,1)S(1)}, u32[]{:S(2)}, u32[]{:S(2)}) collective-permute-start(bf16[1,1,2,1,64,4608]{5,4,3,2,1,0:T(8,128)(2,1)S(1)} %split.245), channel_id=1, source_target_pairs={{0,16},{2,18},{4,20},{6,22},{8,24},{10,26},{12,28},{14,30},{16,0},... | collective-permute-start | bytes 3538952 | tf_op jit(solution)/shard_map/ppermute | solution.py:332
  616.9 40.9 %collective-permute-start.47 = (bf16[2,1,1,1,64,2304]{5,4,3,2,1,0:T(8,128)(2,1)S(1)}, bf16[2,1,1,1,64,2304]{5,4,3,2,1,0:T(8,128)(2,1)S(1)}, u32[]{:S(2)}, u32[]{:S(2)}) collective-permute-start(bf16[2,1,1,1,64,2304]{5,4,3,2,1,0:T(8,128)(2,1)S(1)} %split.227), channel_id=1, source_target_pairs={{0,8},{2,10},{4,12},{6,14},{8,0},{10,2},{12,4},{14,6},{16,24},{18,... | collective-permute-start | bytes 1769480 | tf_op jit(solution)/shard_map/ppermute | solution.py:332
  617.3 55.3 %collective-permute-start.52 = (bf16[2,1,1,1,64,2304]{5,4,3,2,1,0:T(8,128)(2,1)S(1)}, bf16[2,1,1,1,64,2304]{5,4,3,2,1,0:T(8,128)(2,1)S(1)}, u32[]{:S(2)}, u32[]{:S(2)}) collective-permute-start(bf16[2,1,1,1,64,2304]{5,4,3,2,1,0:T(8,128)(2,1)S(1)} %split.237), channel_id=1, source_target_pairs={{0,8},{2,10},{4,12},{6,14},{8,0},{10,2},{12,4},{14,6},{16,24},{18,... | collective-permute-start | bytes 1769480 | tf_op jit(solution)/shard_map/ppermute | solution.py:332
  648.3 25.7 %collective-permute-start.57 = (bf16[1,1,1,1,64,4608]{5,4,3,2,1,0:T(8,128)(2,1)S(1)}, bf16[1,1,1,1,64,4608]{5,4,3,2,1,0:T(8,128)(2,1)S(1)}, u32[]{:S(2)}, u32[]{:S(2)}) collective-permute-start(bf16[1,1,1,1,64,4608]{5,4,3,2,1,0:T(8,128)(2,1)S(1)} %split.247), channel_id=1, source_target_pairs={{0,4},{2,6},{4,0},{6,2},{8,12},{10,14},{12,8},{14,10},{16,20},{18,... | collective-permute-start | bytes 1769480 | tf_op jit(solution)/shard_map/ppermute | solution.py:332
  658.0 17.0 %collective-permute-start.48 = (bf16[1,1,1,1,64,2304]{5,4,3,2,1,0:T(8,128)(2,1)S(1)}, bf16[1,1,1,1,64,2304]{5,4,3,2,1,0:T(8,128)(2,1)S(1)}, u32[]{:S(2)}, u32[]{:S(2)}) collective-permute-start(bf16[1,1,1,1,64,2304]{5,4,3,2,1,0:T(8,128)(2,1)S(1)} %split.229), channel_id=1, source_target_pairs={{0,16},{2,18},{4,20},{6,22},{8,24},{10,26},{12,28},{14,30},{16,0},... | collective-permute-start | bytes 884744 | tf_op jit(solution)/shard_map/ppermute | solution.py:332
  672.8 13.7 %collective-permute-start.53 = (bf16[1,1,1,1,64,2304]{5,4,3,2,1,0:T(8,128)(2,1)S(1)}, bf16[1,1,1,1,64,2304]{5,4,3,2,1,0:T(8,128)(2,1)S(1)}, u32[]{:S(2)}, u32[]{:S(2)}) collective-permute-start(bf16[1,1,1,1,64,2304]{5,4,3,2,1,0:T(8,128)(2,1)S(1)} %split.239), channel_id=1, source_target_pairs={{0,16},{2,18},{4,20},{6,22},{8,24},{10,26},{12,28},{14,30},{16,0},... | collective-permute-start | bytes 884744 | tf_op jit(solution)/shard_map/ppermute | solution.py:332
  674.1 13.2 %collective-permute-start.58 = (bf16[1,1,1,1,64,2304]{5,4,3,2,1,0:T(8,128)(2,1)S(1)}, bf16[1,1,1,1,64,2304]{5,4,3,2,1,0:T(8,128)(2,1)S(1)}, u32[]{:S(2)}, u32[]{:S(2)}) collective-permute-start(bf16[1,1,1,1,64,2304]{5,4,3,2,1,0:T(8,128)(2,1)S(1)} %split.249), channel_id=1, source_target_pairs={{0,1},{1,0},{2,3},{3,2},{4,5},{5,4},{6,7},{7,6},{8,9},{9,8},{10,11... | collective-permute-start | bytes 884744 | tf_op jit(solution)/shard_map/ppermute | solution.py:332
  (129 other events, 1207.8 us)

commit v2 on v1

--- a/solution.py
+++ b/solution.py
@@ -420,10 +420,14 @@
     qkv_full = gather_steps(qkv_part, [last], steps).reshape(D, -1)
     out_full = gather_steps(out_part, [last], steps).reshape(D, -1)
     cot_own = sequence_of(cot_local, side)
-    gate_full, up_full, down_full = (
-        gather_steps(opened(weight, steps), order + [last], steps).reshape(D, -1)
-        for weight, order in zip((gate_local, up_local, down_local.T), orders)
-    )
+    feed = [opened(weight, steps) for weight in (gate_local, up_local, down_local.T)]
+
+    def grow(pieces, first, end=None):
+        return [
+            gather_steps(piece, order[first:end], steps) for piece, order in zip(pieces, orders)
+        ]
+
+    feed = grow(feed, 0, -2)
     features = jnp.arange(D)
     block_rows = D // blocks
     moved = ((features // block_rows) ^ place) * block_rows + features % block_rows
@@ -456,6 +460,8 @@
     inverse_k = norm_stats(key_heads)
     key_b = rotary(key_heads * inverse_k * key_gain, cosine, sine_part).astype(jnp.bfloat16)
     value_b = value_proj.reshape(seq_rows, KV, HD).astype(jnp.bfloat16)
+    feed, query_b, key_b, value_b = lax.optimization_barrier((feed, query_b, key_b, value_b))
+    feed = grow(feed, -2, -1)
     scores = masked_scores(query_b, key_b, allowed, score_scale)
     row_max = jnp.max(scores, axis=-1, keepdims=True)
     log_total = row_max + jnp.log(jnp.sum(jnp.exp(scores - row_max), axis=-1, keepdims=True))
@@ -463,10 +469,16 @@
     attention_b = attention.astype(jnp.bfloat16)
     mixed_b = jnp.einsum("ngqk,knd->qngd", attention_b, value_b, preferred_element_type=jnp.float32)
     mixed_b = mixed_b.reshape(seq_rows, H * HD).astype(jnp.bfloat16)
+    feed, mixed_b = lax.optimization_barrier((feed, mixed_b))
+    feed = grow(feed, -1)
     hidden_one = rows_in + times_t(mixed_b, out_full)
     inverse_two = norm_stats(hidden_one)
     normed_two = (hidden_one * inverse_two * ffn_gain).astype(jnp.bfloat16)
 
+    feed, normed_two = lax.optimization_barrier((feed, normed_two))
+    gate_full, up_full, down_full = (
+        gather_steps(piece, [last], steps).reshape(D, -1) for piece in feed
+    )
     grad_out = cot_b.astype(jnp.float32)
     gate_act = times(normed_two, gate_full)
     up_act = times(normed_two, up_full)
@@ -487,16 +499,29 @@
         grad = scatter_steps(grad.reshape(wide), order, steps)
         return grad.reshape(block_rows, -1).astype(jnp.float32)
 
-    down_grad = scatter_grad(rows_summed(cot_b, inner_b), orders[2])
-    gate_grad = scatter_grad(rows_summed(normed_two, grad_gate), orders[0])
-    up_grad = scatter_grad(rows_summed(normed_two, grad_up), orders[1])
+    def shrink(pieces, first, end=None):
+        return [
+            scatter_steps(piece, order[::-1][first:end], steps)
+            for piece, order in zip(pieces, orders)
+        ]
+
+    feed_grads = [
+        rows_summed(normed_two, grad_gate).reshape(wide),
+        rows_summed(normed_two, grad_up).reshape(wide),
+        rows_summed(cot_b, inner_b).reshape(wide),
+    ]
     grad_normed_two = times_t(grad_gate, gate_full) + times_t(grad_up, up_full)
+    feed_grads, grad_normed_two = lax.optimization_barrier((feed_grads, grad_normed_two))
+    feed_grads = [scatter_steps(grad, [last], steps) for grad in feed_grads]
 
     back_two, ffn_part = norm_back(hidden_one, inverse_two, ffn_gain, grad_normed_two)
     grad_hidden = grad_out + back_two
     grad_attn = grad_hidden.astype(jnp.bfloat16)
-    out_grad = scatter_grad(rows_summed(grad_attn, mixed_b), orders[1])
+    out_sum = rows_summed(grad_attn, mixed_b)
     grad_mixed = times(grad_attn, out_full).astype(jnp.bfloat16)
+    feed_grads, out_sum, grad_mixed = lax.optimization_barrier((feed_grads, out_sum, grad_mixed))
+    feed_grads = shrink(feed_grads, 0, 1)
+    out_grad = scatter_grad(out_sum, orders[1])
     grad_mixed = grad_mixed.reshape(seq_rows, KV, group_size, HD)
     grad_value = jnp.einsum(
         "ngqk,qngd->knd", attention_b, grad_mixed, preferred_element_type=jnp.float32
@@ -508,6 +533,8 @@
         grad_attention - jnp.sum(attention * grad_attention, axis=-1, keepdims=True)
     )
     grad_scores = grad_scores.astype(jnp.bfloat16)
+    feed_grads, grad_scores = lax.optimization_barrier((feed_grads, grad_scores))
+    feed_grads = shrink(feed_grads, 1, 2)
     grad_query = (
         jnp.einsum("ngqk,knd->qngd", grad_scores, key_b, preferred_element_type=jnp.float32)
         * score_scale
@@ -529,6 +556,10 @@
             grad_q[:, q_cols:], grad_k[:, k_cols:], grad_v[:, k_cols:],
         ],
         axis=1,
+    )
+    feed_grads, grad_qkv = lax.optimization_barrier((feed_grads, grad_qkv))
+    gate_grad, up_grad, down_grad = (
+        grad.reshape(block_rows, -1).astype(jnp.float32) for grad in shrink(feed_grads, 2)
     )
     qkv_grad = scatter_grad(rows_summed(normed_b, grad_qkv), orders[0])
     grad_normed = times_t(grad_qkv, qkv_full)

time: 698 us -> 772 us (1.11)
  other arithmetic: 101 us -> 162 us
  waiting for transfers between devices: 279 us -> 295 us
  local copies, waits for them, and re-layouts: 73.7 us -> 87.9 us
  matrix products: 159 us -> 148 us
    sub x0 -> x1, other arithmetic: none -> 26 us  [whole_sequence(): grad_attention - jnp.sum(attention * grad_attention, axis=-1, keepdims=True)]
    concatenate x25, other arithmetic: 31 us -> 56.4 us  [gather_steps(): jnp.concatenate([piece, other], axis=step - 1 if step else piece.ndim - 1)]
    convert_element_type x20, other arithmetic: 22.6 us -> 37.9 us  [scatter_steps(): (kept.astype(jnp.float32) + other.astype(jnp.float32)).astype(values.dtype)]
    split x25, local copies, waits for them, and re-layouts: 14.8 us -> 25.6 us  [scatter_steps(): kept, sent = jnp.split(values, 2, axis=axis)]
    ppermute x55, waiting for transfers between devices: 269 us -> 279 us  [exchange(): return lax.ppermute(values, name, pairs)]
    ppermute x55, starting transfers between devices: 68.7 us -> 59.7 us  [exchange(): return lax.ppermute(values, name, pairs)]
    unnamed x275 -> x233, local copies, waits for them, and re-layouts: 15.6 us -> 11.3 us
  transfers between devices with their start and end apart: 59 -> 59, of which waited for: 31 -> 26; matrix products, arithmetic and copies ran while one was open for 24% -> 39% of each run, Pallas kernels for 0% -> 0%
where the time goes in v2:
time: 772 us; the launch traced here: 762 us
  waiting for transfers between devices  295 us (38%)
  other arithmetic  162 us (21%)
  matrix products  148 us (19%)
  local copies, waits for them, and re-layouts  87.9 us (11%)
  starting transfers between devices  66.1 us (9%)
    ppermute x55, waiting for transfers between devices, exchange(): return lax.ppermute(values, name, pairs)  279 us
    dot_general x10, matrix products, times(): return jnp.dot(left, right, preferred_element_type=jnp.float32)  64.2 us
    ppermute x55, starting transfers between devices, exchange(): return lax.ppermute(values, name, pairs)  59.7 us
    concatenate x25, other arithmetic, gather_steps(): jnp.concatenate([piece, other], axis=step - 1 if step else piece.ndim - 1)  56.4 us
    convert_element_type x20, other arithmetic, scatter_steps(): (kept.astype(jnp.float32) + other.astype(jnp.float32)).astype(values.dtype)  37.9 us
    sub x1, other arithmetic, whole_sequence(): grad_attention - jnp.sum(attention * grad_attention, axis=-1, keepdims=True)  26 us
    dot_general x5, matrix products, rows_summed(): lax.dot_general(left, right, (((0,), (0,)), ((), ())), preferred_element_...  25.8 us
    split x25, local copies, waits for them, and re-layouts, scatter_steps(): kept, sent = jnp.split(values, 2, axis=axis)  25.6 us
  transfers between devices with their start and end apart: 59, of which 26 were waited for; matrix products, arithmetic and copies ran while one was open for 39% of the time, Pallas kernels for 0%

profile of v2, /device:TPU:0, one launch (start us, length us, event | category | flops | bytes accessed | tf_op | source)
XLA Modules:
  0.0 762.3 jit_solution(16592715578095098512)
XLA Ops:
  1.6 4.1 collective-permute-start.1
  10.3 3.8 collective-permute-done.1
  14.7 6.3 collective-permute-done.2
  29.1 3.9 collective-permute-done.3
  39.3 8.1 %collective-permute-done.8 = bf16[2,2,1,1,64,1024]{5,4,3,2,1,0:T(8,128)(2,1)} collective-permute-done((bf16[2,2,1,1,64,1024]{5,4,3,2,1,0:T(8,128)(2,1)}, bf16[2,2,1,1,64,1024]{5,4,3,2,1,0:T(8,128)(2,1)}, u32[]{:S(2)}, u32[]{:S(2)}) %collective-permute-start.8) | collective-permute-done | bytes 524320 | tf_op jit(solution)/shard_map/ppermute | solution.py:332
  49.6 6.9 collective-permute-done.4
  57.9 5.0 collective-permute-start.11
  66.1 14.5 %collective-permute-done.11 = bf16[1,1,1,1,64,2304]{5,4,3,2,1,0:T(8,128)(2,1)S(1)} collective-permute-done((bf16[1,1,1,1,64,2304]{5,4,3,2,1,0:T(8,128)(2,1)S(1)}, bf16[1,1,1,1,64,2304]{5,4,3,2,1,0:T(8,128)(2,1)S(1)}, u32[]{:S(2)}, u32[]{:S(2)}) %collective-permute-start.11) | collective-permute-done | bytes 294944 | tf_op jit(solution)/shard_map/ppermute | solution.py:332
  81.3 5.4 collective-permute-done.9
  88.5 10.8 %collective-permute-done.12 = bf16[2,1,1,1,64,2304]{5,4,3,2,1,0:T(8,128)(2,1)S(1)} collective-permute-done((bf16[2,1,1,1,64,2304]{5,4,3,2,1,0:T(8,128)(2,1)S(1)}, bf16[2,1,1,1,64,2304]{5,4,3,2,1,0:T(8,128)(2,1)S(1)}, u32[]{:S(2)}, u32[]{:S(2)}) %collective-permute-start.12) | collective-permute-done | bytes 589856 | tf_op jit(solution)/shard_map/ppermute | solution.py:332
  100.6 11.4 %collective-permute-done.10 = bf16[2,1,1,1,64,2304]{5,4,3,2,1,0:T(8,128)(2,1)S(1)} collective-permute-done((bf16[2,1,1,1,64,2304]{5,4,3,2,1,0:T(8,128)(2,1)S(1)}, bf16[2,1,1,1,64,2304]{5,4,3,2,1,0:T(8,128)(2,1)S(1)}, u32[]{:S(2)}, u32[]{:S(2)}) %collective-permute-start.10) | collective-permute-done | bytes 589856 | tf_op jit(solution)/shard_map/ppermute | solution.py:332
  134.3 7.5 fusion.111
  141.9 8.3 %exponential_reduce_fusion = f32[8,2,512]{2,1,0:T(2,128)S(1)} fusion(f32[8,2,512,512]{2,3,1,0:T(8,128)} %get-tuple-element.146, f32[8,2,512]{2,1,0:T(2,128)S(1)} %get-tuple-element.145), kind=kLoop, calls=%fused_computation.11 | loop fusion | flops 8380416 | bytes 16842752 | tf_op jit(solution)/shard_map/reduce_sum | solution.py:467
  150.2 8.5 %fusion.39 = bf16[8,64,2,512]{3,1,2,0:T(8,128)(2,1)S(1)} fusion(f32[8,2,512,512]{2,3,1,0:T(8,128)} %get-tuple-element.146, f32[8,2,512]{2,1,0:T(2,128)S(1)} %bitcast.266, bf16[512,8,64]{0,2,1:T(8,128)(2,1)S(1)} %bitcast.226), kind=kOutput, calls=%fused_computation.104 | convolution fusion | flops 545783808 | bytes 18382848 | tf_op jit(solution)/shard_map/ngqk,knd->qngd/dot_general | solution.py:470
  158.7 25.7 %collective-permute-done.18 = bf16[1,1,2,1,64,4608]{5,4,3,2,1,0:T(8,128)(2,1)} collective-permute-done((bf16[1,1,2,1,64,4608]{5,4,3,2,1,0:T(8,128)(2,1)S(1)}, bf16[1,1,2,1,64,4608]{5,4,3,2,1,0:T(8,128)(2,1)}, u32[]{:S(2)}, u32[]{:S(2)}) %collective-permute-start.18) | collective-permute-done | bytes 1179680 | tf_op jit(solution)/shard_map/ppermute | solution.py:332
  184.4 3.0 pad_maximum_fusion.9
  187.4 2.8 pad_maximum_fusion.8
  190.2 3.0 pad_maximum_fusion.7
  198.3 48.2 %collective-permute-done.22 = bf16[2,1,2,1,64,4608]{5,4,3,2,1,0:T(8,128)(2,1)} collective-permute-done((bf16[2,1,2,1,64,4608]{5,4,3,2,1,0:T(8,128)(2,1)}, bf16[2,1,2,1,64,4608]{5,4,3,2,1,0:T(8,128)(2,1)}, u32[]{:S(2)}, u32[]{:S(2)}) %collective-permute-start.22) | collective-permute-done | bytes 2359328 | tf_op jit(solution)/shard_map/ppermute | solution.py:332
  246.5 4.9 pad_maximum_fusion.5
  251.4 2.8 pad_maximum_fusion.4
  254.3 6.0 pad_maximum_fusion.3
  262.4 12.4 %collective-permute-done.27 = bf16[256,1024]{1,0:T(8,128)(2,1)S(1)} collective-permute-done((bf16[256,1024]{1,0:T(8,128)(2,1)S(1)}, bf16[256,1024]{1,0:T(8,128)(2,1)S(1)}, u32[]{:S(2)}, u32[]{:S(2)}) %collective-permute-start.27) | collective-permute-done | bytes 524320 | tf_op jit(solution)/shard_map/ppermute | solution.py:303
  277.3 8.2 %pad_maximum_fusion.1 = bf16[2,2,2,2,64,4608]{5,4,3,2,1,0:T(8,128)(2,1)} fusion(bf16[2,2,2,1,64,4608]{5,4,3,2,1,0:T(8,128)(2,1)} %collective-permute-done.24, bf16[2,2,2,1,64,4608]{5,4,3,2,1,0:T(8,128)(2,1)} %copy-done.4), kind=kLoop, calls=%fused_computation.17 | loop fusion | flops 4718592 | bytes 18874368 | tf_op jit(solution)/shard_map/concatenate | solution.py:344
  285.5 8.7 %pad_maximum_fusion = bf16[2,2,2,2,64,4608]{5,4,3,2,1,0:T(8,128)(2,1)} fusion(bf16[2,2,2,1,64,4608]{5,4,3,2,1,0:T(8,128)(2,1)} %collective-permute-done.23, bf16[2,2,2,1,64,4608]{5,4,3,2,1,0:T(8,128)(2,1)} %pad_maximum_fusion.3), kind=kLoop, calls=%fused_computation.16 | loop fusion | flops 4718592 | bytes 18874368 | tf_op jit(solution)/shard_map/concatenate | solution.py:344
  294.2 11.2 %fusion.113 = f32[512,4608]{1,0:T(8,128)} fusion(bf16[512,1024]{1,0:T(8,128)(2,1)S(1)} %multiply_convert_fusion.3, bf16[1024,4608]{1,0:T(8,128)(2,1)} %bitcast.216), kind=kOutput, calls=%fused_computation.263 | convolution fusion | flops 4831838208 | bytes 19922944 | tf_op jit(solution)/shard_map/dot_general | solution.py:367
  305.4 7.4 fusion.112
  312.8 8.2 %pad_maximum_fusion.2 = bf16[2,2,2,2,64,4608]{5,4,3,2,1,0:T(8,128)(2,1)} fusion(bf16[2,2,2,1,64,4608]{5,4,3,2,1,0:T(8,128)(2,1)} %collective-permute-done.25, bf16[2,2,2,1,64,4608]{5,4,3,2,1,0:T(8,128)(2,1)} %pad_maximum_fusion.5), kind=kLoop, calls=%fused_computation.18 | loop fusion | flops 4718592 | bytes 18874368 | tf_op jit(solution)/shard_map/concatenate | solution.py:344
  321.0 17.8 %multiply_convert_fusion = (bf16[512,4608]{1,0:T(8,128)(2,1)}, bf16[512,4608]{1,0:T(8,128)(2,1)}, bf16[512,4608]{1,0:T(8,128)(2,1)}) fusion(f32[512,4608]{1,0:T(8,128)} %fusion.112, f32[512,4608]{1,0:T(8,128)} %fusion.113, bf16[512,1024]{1,0:T(8,128)(2,1)} %fusion.38, bf16[1024,4608]{1,0:T(8,128)(2,1)} %bitcast.214), kind=kOutput, calls=%fused_computation.22 | convolution fusion | flops 4869586944 | bytes 43515904 | tf_op jit(solution)/shard_map/dot_general | solution.py:367
  338.8 9.2 %fusion.114 = f32[512,1024]{1,0:T(8,128)S(1)} fusion(bf16[512,4608]{1,0:T(8,128)(2,1)} %get-tuple-element.98, bf16[1024,4608]{1,0:T(8,128)(2,1)} %bitcast.217), kind=kOutput, calls=%fused_computation.264 | convolution fusion | flops 4831838208 | bytes 16252928 | tf_op jit(solution)/shard_map/dot_general | solution.py:371
  348.0 7.8 %convolution_convert_fusion.1 = bf16[1024,4608]{1,0:T(8,128)(2,1)} fusion(bf16[512,1024]{1,0:T(8,128)(2,1)S(1)} %multiply_convert_fusion.3, bf16[512,4608]{1,0:T(8,128)(2,1)S(1)} %copy-done.95), kind=kOutput, calls=%fused_computation.14 | convolution fusion | flops 4836556800 | bytes 15204352 | tf_op jit(solution)/shard_map/dot_general | solution.py:377
  355.8 7.5 convolution_convert_fusion.2
  363.4 6.4 convolution_add_fusion
  369.7 5.4 convolution_convert_fusion
  394.8 3.3 copy.82
  398.1 4.8 split.153
  403.4 4.8 split.151
  408.1 12.4 %fusion.37 = bf16[512,1024]{1,0:T(8,128)(2,1)} fusion(s32[1024]{0:T(1024)S(1)} %copy-done.83, f32[512,1024]{1,0:T(8,128)S(1)} %get-tuple-element.148, bf16[512,4608]{1,0:T(8,128)(2,1)} %get-tuple-element.100, bf16[1024,4608]{1,0:T(8,128)(2,1)} %bitcast.215), kind=kOutput, calls=%fused_computation.101 | convolution fusion | flops 5908201472 | bytes 17305600 | tf_op jit(solution)/shard_map/dot_general | solution.py:367
  427.4 2.7 subtract_add_fusion
  435.1 5.9 add_convert_fusion
  441.0 7.3 add_convert_fusion.1
  448.3 6.0 add_convert_fusion.2
  458.7 3.3 split.161
  462.3 8.2 %fusion.67 = f32[8,512,512,2]{2,1,3,0:T(8,128)} fusion(bf16[512,8,2,64]{0,3,2,1:T(8,128)(2,1)S(1)} %bitcast.202, bf16[512,8,64]{0,2,1:T(8,128)(2,1)S(1)} %bitcast.227), kind=kOutput, calls=%fused_computation.166 | convolution fusion | flops 536870912 | bytes 18350080 | tf_op jit(solution)/shard_map/qngd,knd->ngqk/dot_general | solution.py:529
  473.8 26.0 %fusion.2 = bf16[8,2,512,512]{2,3,1,0:T(8,128)(2,1)} fusion(f32[8,512,512,2]{2,1,3,0:T(8,128)} %fusion.67, f32[8,2,512,512]{2,3,1,0:T(8,128)} %get-tuple-element.146, f32[8,2,512]{2,1,0:T(2,128)S(1)} %bitcast.267), kind=kOutput, calls=%fused_computation.8 | output fusion | flops 25174528 | bytes 41975808 | tf_op jit(solution)/shard_map/sub | solution.py:533
  503.0 8.4 %fusion.47 = bf16[8,64,512]{2,1,0:T(8,128)(2,1)S(1)} fusion(bf16[512,8,2,64]{0,3,2,1:T(8,128)(2,1)S(1)} %bitcast.203, f32[8,2,512,512]{2,3,1,0:T(8,128)} %get-tuple-element.146, f32[8,2,512]{2,1,0:T(2,128)S(1)} %bitcast.268), kind=kOutput, calls=%fused_computation.111 | convolution fusion | flops 545521664 | bytes 18382848 | tf_op jit(solution)/shard_map/ngqk,qngd->knd/dot_general | solution.py:526
  514.2 3.2 split.157
  520.7 4.5 add_convert_fusion.3
  525.2 29.3 %collective-permute-done.32 = bf16[2,2,1,1,64,4608]{5,4,3,2,1,0:T(8,128)(2,1)} collective-permute-done((bf16[2,2,1,1,64,4608]{5,4,3,2,1,0:T(8,128)(2,1)}, bf16[2,2,1,1,64,4608]{5,4,3,2,1,0:T(8,128)(2,1)}, u32[]{:S(2)}, u32[]{:S(2)}) %collective-permute-start.32) | collective-permute-done | bytes 2359328 | tf_op jit(solution)/shard_map/ppermute | solution.py:332
  554.5 3.6 add_convert_fusion.4
  558.1 11.5 %collective-permute-done.31 = bf16[2,2,2,1,64,2304]{5,4,3,2,1,0:T(8,128)(2,1)} collective-permute-done((bf16[2,2,2,1,64,2304]{5,4,3,2,1,0:T(8,128)(2,1)}, bf16[2,2,2,1,64,2304]{5,4,3,2,1,0:T(8,128)(2,1)}, u32[]{:S(2)}, u32[]{:S(2)}) %collective-permute-start.31) | collective-permute-done | bytes 2359328 | tf_op jit(solution)/shard_map/ppermute | solution.py:332
  569.6 4.3 add_convert_fusion.5
  593.3 2.9 copy.86
  610.8 15.4 %collective-permute-done.35 = bf16[2,2,1,1,64,2304]{5,4,3,2,1,0:T(8,128)(2,1)S(1)} collective-permute-done((bf16[2,2,1,1,64,2304]{5,4,3,2,1,0:T(8,128)(2,1)S(1)}, bf16[2,2,1,1,64,2304]{5,4,3,2,1,0:T(8,128)(2,1)S(1)}, u32[]{:S(2)}, u32[]{:S(2)}) %collective-permute-start.35) | collective-permute-done | bytes 1179680 | tf_op jit(solution)/shard_map/ppermute | solution.py:332
  626.6 24.8 %collective-permute-done.36 = bf16[1,1,2,1,64,4608]{5,4,3,2,1,0:T(8,128)(2,1)S(1)} collective-permute-done((bf16[1,1,2,1,64,4608]{5,4,3,2,1,0:T(8,128)(2,1)S(1)}, bf16[1,1,2,1,64,4608]{5,4,3,2,1,0:T(8,128)(2,1)S(1)}, u32[]{:S(2)}, u32[]{:S(2)}) %collective-permute-start.36) | collective-permute-done | bytes 1179680 | tf_op jit(solution)/shard_map/ppermute | solution.py:332
  655.4 4.6 fusion.27
  670.9 4.7 fusion.5
  691.2 3.7 collective-permute-done.37
  696.6 5.3 collective-permute-done.57
  708.7 13.5 %collective-permute-done.53 = bf16[2,1,1,1,64,2304]{5,4,3,2,1,0:T(8,128)(2,1)S(1)} collective-permute-done((bf16[2,1,1,1,64,2304]{5,4,3,2,1,0:T(8,128)(2,1)S(1)}, bf16[2,1,1,1,64,2304]{5,4,3,2,1,0:T(8,128)(2,1)S(1)}, u32[]{:S(2)}, u32[]{:S(2)}) %collective-permute-start.53) | collective-permute-done | bytes 589856 | tf_op jit(solution)/shard_map/ppermute | solution.py:332
  722.5 10.7 %collective-permute-done.44 = bf16[2,2,2,1,64,1024]{5,4,3,2,1,0:T(8,128)(2,1)S(1)} collective-permute-done((bf16[2,2,2,1,64,1024]{5,4,3,2,1,0:T(8,128)(2,1)S(1)}, bf16[2,2,2,1,64,1024]{5,4,3,2,1,0:T(8,128)(2,1)S(1)}, u32[]{:S(2)}, u32[]{:S(2)}) %collective-permute-start.44) | collective-permute-done | bytes 1048608 | tf_op jit(solution)/shard_map/ppermute | solution.py:332
  736.2 10.2 %collective-permute-done.45 = bf16[2,2,1,1,64,1024]{5,4,3,2,1,0:T(8,128)(2,1)S(1)} collective-permute-done((bf16[2,2,1,1,64,1024]{5,4,3,2,1,0:T(8,128)(2,1)S(1)}, bf16[2,2,1,1,64,1024]{5,4,3,2,1,0:T(8,128)(2,1)S(1)}, u32[]{:S(2)}, u32[]{:S(2)}) %collective-permute-start.45) | collective-permute-done | bytes 524320 | tf_op jit(solution)/shard_map/ppermute | solution.py:332
  749.1 4.0 collective-permute-done.46
  755.9 4.6 collective-permute-done.47
  (498 shorter events, 194.0 us)
Async XLA Ops:
  1.6 12.5 %collective-permute-start.1 = (bf16[1,1,1,1,64,1024]{5,4,3,2,1,0:T(8,128)(2,1)S(1)}, bf16[1,1,1,1,64,1024]{5,4,3,2,1,0:T(8,128)(2,1)S(1)}, u32[]{:S(2)}, u32[]{:S(2)}) collective-permute-start(bf16[1,1,1,1,64,1024]{5,4,3,2,1,0:T(8,128)(2,1)S(1)} %maximum_bitcast_fusion), channel_id=1, source_target_pairs={{0,16},{2,18},{4,20},{6,22},{8,24},{10,26},{12,28},{14,30},{16,0},... | collective-permute-start | bytes 393224 | tf_op jit(solution)/shard_map/ppermute | solution.py:332
  5.7 16.7 %collective-permute-start.5 = (bf16[1,1,1,1,64,512]{5,4,3,2,1,0:T(8,128)(2,1)}, bf16[1,1,1,1,64,512]{5,4,3,2,1,0:T(8,128)(2,1)S(1)}, u32[]{:S(2)}, u32[]{:S(2)}) collective-permute-start(bf16[1,1,1,1,64,512]{5,4,3,2,1,0:T(8,128)(2,1)} %bitcast.259), channel_id=1, source_target_pairs={{0,16},{2,18},{4,20},{6,22},{8,24},{10,26},{12,28},{14,30},{16,0},... | collective-permute-start | bytes 196616 | tf_op jit(solution)/shard_map/ppermute | solution.py:332
  7.7 30.4 %collective-permute-start = (bf16[256,1024]{1,0:T(8,128)(2,1)}, bf16[256,1024]{1,0:T(8,128)(2,1)}, u32[]{:S(2)}, u32[]{:S(2)}) collective-permute-start(bf16[256,1024]{1,0:T(8,128)(2,1)} %dynamic-slice_bitcast_fusion.2), channel_id=1, source_target_pairs={{0,1},{1,0},{2,3},{3,2},{4,5},{5,4},{6,7},{7,6},{8,9},{9,8},{10,11... | collective-permute-start | bytes 1572872 | tf_op jit(solution)/shard_map/ppermute | solution.py:303
  14.1 6.9 collective-permute-start.2
  14.7 114.3 %copy-start.44 = (f32[512,32]{0,1:T(8,128)}, f32[512,32]{0,1:T(8,128)S(1)}, u32[]{:S(2)}) copy-start(f32[512,32]{0,1:T(8,128)S(1)} %get-tuple-element.133) | copy-start | bytes 196612
  14.7 114.3 %copy-start.46 = (f32[512,32]{0,1:T(8,128)}, f32[512,32]{0,1:T(8,128)S(1)}, u32[]{:S(2)}) copy-start(f32[512,32]{0,1:T(8,128)S(1)} %get-tuple-element.134) | copy-start | bytes 196612
  21.1 11.9 %collective-permute-start.3 = (bf16[2,2,1,1,64,1024]{5,4,3,2,1,0:T(8,128)(2,1)S(1)}, bf16[2,2,1,1,64,1024]{5,4,3,2,1,0:T(8,128)(2,1)S(1)}, u32[]{:S(2)}, u32[]{:S(2)}) collective-permute-start(bf16[2,2,1,1,64,1024]{5,4,3,2,1,0:T(8,128)(2,1)S(1)} %pad_maximum_fusion.27), channel_id=1, source_target_pairs={{0,4},{2,6},{4,0},{6,2},{8,12},{10,14},{12,8},{14,10},{16,20},{18,... | collective-permute-start | bytes 1572872 | tf_op jit(solution)/shard_map/ppermute | solution.py:332
  22.4 5.0 collective-permute-start.6
  27.5 7.8 %collective-permute-start.7 = (bf16[2,2,1,1,64,512]{5,4,3,2,1,0:T(8,128)(2,1)S(1)}, bf16[2,2,1,1,64,512]{5,4,3,2,1,0:T(8,128)(2,1)S(1)}, u32[]{:S(2)}, u32[]{:S(2)}) collective-permute-start(bf16[2,2,1,1,64,512]{5,4,3,2,1,0:T(8,128)(2,1)S(1)} %pad_maximum_fusion.32), channel_id=1, source_target_pairs={{0,1},{1,0},{2,3},{3,2},{4,5},{5,4},{6,7},{7,6},{8,9},{9,8},{10,11... | collective-permute-start | bytes 786440 | tf_op jit(solution)/shard_map/ppermute | solution.py:332
  33.1 23.4 %collective-permute-start.4 = (bf16[2,2,2,1,64,1024]{5,4,3,2,1,0:T(8,128)(2,1)S(1)}, bf16[2,2,2,1,64,1024]{5,4,3,2,1,0:T(8,128)(2,1)}, u32[]{:S(2)}, u32[]{:S(2)}) collective-permute-start(bf16[2,2,2,1,64,1024]{5,4,3,2,1,0:T(8,128)(2,1)S(1)} %pad_maximum_fusion.18), channel_id=1, source_target_pairs={{0,1},{1,0},{2,3},{3,2},{4,5},{5,4},{6,7},{7,6},{8,9},{9,8},{10,11... | collective-permute-start | bytes 3145736 | tf_op jit(solution)/shard_map/ppermute | solution.py:332
  36.2 11.2 %collective-permute-start.8 = (bf16[2,2,1,1,64,1024]{5,4,3,2,1,0:T(8,128)(2,1)}, bf16[2,2,1,1,64,1024]{5,4,3,2,1,0:T(8,128)(2,1)}, u32[]{:S(2)}, u32[]{:S(2)}) collective-permute-start(bf16[2,2,1,1,64,1024]{5,4,3,2,1,0:T(8,128)(2,1)} %pad_maximum_fusion.28), channel_id=1, source_target_pairs={{0,4},{2,6},{4,0},{6,2},{8,12},{10,14},{12,8},{14,10},{16,20},{18,... | collective-permute-start | bytes 1572872 | tf_op jit(solution)/shard_map/ppermute | solution.py:332
  37.8 76.8 %copy-start.79 = (f32[1024]{0:T(1024)}, f32[1024]{0:T(1024)S(1)}, u32[]{:S(2)}) copy-start(f32[1024]{0:T(1024)S(1)} %mul.516) | copy-start | bytes 12292
  57.9 22.8 %collective-permute-start.11 = (bf16[1,1,1,1,64,2304]{5,4,3,2,1,0:T(8,128)(2,1)S(1)}, bf16[1,1,1,1,64,2304]{5,4,3,2,1,0:T(8,128)(2,1)S(1)}, u32[]{:S(2)}, u32[]{:S(2)}) collective-permute-start(bf16[1,1,1,1,64,2304]{5,4,3,2,1,0:T(8,128)(2,1)S(1)} %bitcast.246), channel_id=1, source_target_pairs={{0,16},{2,18},{4,20},{6,22},{8,24},{10,26},{12,28},{14,30},{16,0},... | collective-permute-start | bytes 884744 | tf_op jit(solution)/shard_map/ppermute | solution.py:332
  64.4 50.2 %copy-start.90 = (bf16[512,1024]{1,0:T(8,128)(2,1)}, bf16[512,1024]{1,0:T(8,128)(2,1)S(1)}, u32[]{:S(2)}) copy-start(bf16[512,1024]{1,0:T(8,128)(2,1)S(1)} %get-tuple-element.142) | copy-start | bytes 3145732
  64.4 49.8 %collective-permute-start.15 = (bf16[2,2,2,1,64,2048]{5,4,3,2,1,0:T(8,128)(2,1)S(1)}, bf16[2,2,2,1,64,2048]{5,4,3,2,1,0:T(8,128)(2,1)S(1)}, u32[]{:S(2)}, u32[]{:S(2)}) collective-permute-start(bf16[2,2,2,1,64,2048]{5,4,3,2,1,0:T(8,128)(2,1)S(1)} %pad_maximum_fusion.10), channel_id=1, source_target_pairs={{0,2},{2,0},{4,6},{6,4},{8,10},{10,8},{12,14},{14,12},{16,18},{18,... | collective-permute-start | bytes 6291464 | tf_op jit(solution)/shard_map/ppermute | solution.py:332
  64.5 22.4 %collective-permute-start.13 = (bf16[1,1,1,1,64,2304]{5,4,3,2,1,0:T(8,128)(2,1)S(1)}, bf16[1,1,1,1,64,2304]{5,4,3,2,1,0:T(8,128)(2,1)S(1)}, u32[]{:S(2)}, u32[]{:S(2)}) collective-permute-start(bf16[1,1,1,1,64,2304]{5,4,3,2,1,0:T(8,128)(2,1)S(1)} %bitcast.252), channel_id=1, source_target_pairs={{0,1},{1,0},{2,3},{3,2},{4,5},{5,4},{6,7},{7,6},{8,9},{9,8},{10,11... | collective-permute-start | bytes 884744 | tf_op jit(solution)/shard_map/ppermute | solution.py:332
  66.1 20.7 %collective-permute-start.9 = (bf16[1,1,1,1,64,2304]{5,4,3,2,1,0:T(8,128)(2,1)S(1)}, bf16[1,1,1,1,64,2304]{5,4,3,2,1,0:T(8,128)(2,1)S(1)}, u32[]{:S(2)}, u32[]{:S(2)}) collective-permute-start(bf16[1,1,1,1,64,2304]{5,4,3,2,1,0:T(8,128)(2,1)S(1)} %bitcast.249), channel_id=1, source_target_pairs={{0,16},{2,18},{4,20},{6,22},{8,24},{10,26},{12,28},{14,30},{16,0},... | collective-permute-start | bytes 884744 | tf_op jit(solution)/shard_map/ppermute | solution.py:332
  80.7 18.7 %collective-permute-start.12 = (bf16[2,1,1,1,64,2304]{5,4,3,2,1,0:T(8,128)(2,1)S(1)}, bf16[2,1,1,1,64,2304]{5,4,3,2,1,0:T(8,128)(2,1)S(1)}, u32[]{:S(2)}, u32[]{:S(2)}) collective-permute-start(bf16[2,1,1,1,64,2304]{5,4,3,2,1,0:T(8,128)(2,1)S(1)} %pad_maximum_fusion.25), channel_id=1, source_target_pairs={{0,8},{2,10},{4,12},{6,14},{8,0},{10,2},{12,4},{14,6},{16,24},{18,... | collective-permute-start | bytes 1769480 | tf_op jit(solution)/shard_map/ppermute | solution.py:332
  86.8 25.1 %collective-permute-start.10 = (bf16[2,1,1,1,64,2304]{5,4,3,2,1,0:T(8,128)(2,1)S(1)}, bf16[2,1,1,1,64,2304]{5,4,3,2,1,0:T(8,128)(2,1)S(1)}, u32[]{:S(2)}, u32[]{:S(2)}) collective-permute-start(bf16[2,1,1,1,64,2304]{5,4,3,2,1,0:T(8,128)(2,1)S(1)} %pad_maximum_fusion.24), channel_id=1, source_target_pairs={{0,8},{2,10},{4,12},{6,14},{8,0},{10,2},{12,4},{14,6},{16,24},{18,... | collective-permute-start | bytes 1769480 | tf_op jit(solution)/shard_map/ppermute | solution.py:332
  87.0 26.1 %collective-permute-start.14 = (bf16[1,1,1,1,64,4608]{5,4,3,2,1,0:T(8,128)(2,1)S(1)}, bf16[1,1,1,1,64,4608]{5,4,3,2,1,0:T(8,128)(2,1)S(1)}, u32[]{:S(2)}, u32[]{:S(2)}) collective-permute-start(bf16[1,1,1,1,64,4608]{5,4,3,2,1,0:T(8,128)(2,1)S(1)} %pad_maximum_fusion.26), channel_id=1, source_target_pairs={{0,4},{2,6},{4,0},{6,2},{8,12},{10,14},{12,8},{14,10},{16,20},{18,... | collective-permute-start | bytes 1769480 | tf_op jit(solution)/shard_map/ppermute | solution.py:332
  130.3 54.2 %collective-permute-start.18 = (bf16[1,1,2,1,64,4608]{5,4,3,2,1,0:T(8,128)(2,1)S(1)}, bf16[1,1,2,1,64,4608]{5,4,3,2,1,0:T(8,128)(2,1)}, u32[]{:S(2)}, u32[]{:S(2)}) collective-permute-start(bf16[1,1,2,1,64,4608]{5,4,3,2,1,0:T(8,128)(2,1)S(1)} %copy-done.28), channel_id=1, source_target_pairs={{0,16},{2,18},{4,20},{6,22},{8,24},{10,26},{12,28},{14,30},{16,0},... | collective-permute-start | bytes 3538952 | tf_op jit(solution)/shard_map/ppermute | solution.py:332
  131.3 56.1 %collective-permute-start.17 = (bf16[2,2,1,1,64,2304]{5,4,3,2,1,0:T(8,128)(2,1)S(1)}, bf16[2,2,1,1,64,2304]{5,4,3,2,1,0:T(8,128)(2,1)}, u32[]{:S(2)}, u32[]{:S(2)}) collective-permute-start(bf16[2,2,1,1,64,2304]{5,4,3,2,1,0:T(8,128)(2,1)S(1)} %copy-done.26), channel_id=1, source_target_pairs={{0,1},{1,0},{2,3},{3,2},{4,5},{5,4},{6,7},{7,6},{8,9},{9,8},{10,11... | collective-permute-start | bytes 3538952 | tf_op jit(solution)/shard_map/ppermute | solution.py:332
  132.8 57.4 %collective-permute-start.16 = (bf16[2,2,1,1,64,2304]{5,4,3,2,1,0:T(8,128)(2,1)S(1)}, bf16[2,2,1,1,64,2304]{5,4,3,2,1,0:T(8,128)(2,1)}, u32[]{:S(2)}, u32[]{:S(2)}) collective-permute-start(bf16[2,2,1,1,64,2304]{5,4,3,2,1,0:T(8,128)(2,1)S(1)} %copy-done.27), channel_id=1, source_target_pairs={{0,4},{2,6},{4,0},{6,2},{8,12},{10,14},{12,8},{14,10},{16,20},{18,... | collective-permute-start | bytes 3538952 | tf_op jit(solution)/shard_map/ppermute | solution.py:332
  193.2 53.3 %collective-permute-start.22 = (bf16[2,1,2,1,64,4608]{5,4,3,2,1,0:T(8,128)(2,1)}, bf16[2,1,2,1,64,4608]{5,4,3,2,1,0:T(8,128)(2,1)}, u32[]{:S(2)}, u32[]{:S(2)}) collective-permute-start(bf16[2,1,2,1,64,4608]{5,4,3,2,1,0:T(8,128)(2,1)} %pad_maximum_fusion.9), channel_id=1, source_target_pairs={{0,8},{2,10},{4,12},{6,14},{8,0},{10,2},{12,4},{14,6},{16,24},{18,... | collective-permute-start | bytes 7077896 | tf_op jit(solution)/shard_map/ppermute | solution.py:332
  193.2 3.2 collective-permute-start.19
  193.2 58.2 %collective-permute-start.21 = (bf16[2,2,1,1,64,4608]{5,4,3,2,1,0:T(8,128)(2,1)}, bf16[2,2,1,1,64,4608]{5,4,3,2,1,0:T(8,128)(2,1)}, u32[]{:S(2)}, u32[]{:S(2)}) collective-permute-start(bf16[2,2,1,1,64,4608]{5,4,3,2,1,0:T(8,128)(2,1)} %pad_maximum_fusion.8), channel_id=1, source_target_pairs={{0,4},{2,6},{4,0},{6,2},{8,12},{10,14},{12,8},{14,10},{16,20},{18,... | collective-permute-start | bytes 7077896 | tf_op jit(solution)/shard_map/ppermute | solution.py:332
  194.9 59.4 %collective-permute-start.20 = (bf16[2,2,2,1,64,2304]{5,4,3,2,1,0:T(8,128)(2,1)}, bf16[2,2,2,1,64,2304]{5,4,3,2,1,0:T(8,128)(2,1)S(1)}, u32[]{:S(2)}, u32[]{:S(2)}) collective-permute-start(bf16[2,2,2,1,64,2304]{5,4,3,2,1,0:T(8,128)(2,1)} %pad_maximum_fusion.7), channel_id=1, source_target_pairs={{0,1},{1,0},{2,3},{3,2},{4,5},{5,4},{6,7},{7,6},{8,9},{9,8},{10,11... | collective-permute-start | bytes 7077896 | tf_op jit(solution)/shard_map/ppermute | solution.py:332
  260.3 17.0 %collective-permute-start.24 = (bf16[2,2,2,1,64,4608]{5,4,3,2,1,0:T(8,128)(2,1)S(1)}, bf16[2,2,2,1,64,4608]{5,4,3,2,1,0:T(8,128)(2,1)}, u32[]{:S(2)}, u32[]{:S(2)}) collective-permute-start(bf16[2,2,2,1,64,4608]{5,4,3,2,1,0:T(8,128)(2,1)S(1)} %pad_maximum_fusion.4), channel_id=1, source_target_pairs={{0,2},{2,0},{4,6},{6,4},{8,10},{10,8},{12,14},{14,12},{16,18},{18,... | collective-permute-start | bytes 14155784 | tf_op jit(solution)/shard_map/ppermute | solution.py:332
  260.3 25.2 %collective-permute-start.23 = (bf16[2,2,2,1,64,4608]{5,4,3,2,1,0:T(8,128)(2,1)}, bf16[2,2,2,1,64,4608]{5,4,3,2,1,0:T(8,128)(2,1)}, u32[]{:S(2)}, u32[]{:S(2)}) collective-permute-start(bf16[2,2,2,1,64,4608]{5,4,3,2,1,0:T(8,128)(2,1)} %pad_maximum_fusion.3), channel_id=1, source_target_pairs={{0,2},{2,0},{4,6},{6,4},{8,10},{10,8},{12,14},{14,12},{16,18},{18,... | collective-permute-start | bytes 14155784 | tf_op jit(solution)/shard_map/ppermute | solution.py:332
  260.9 14.0 %collective-permute-start.27 = (bf16[256,1024]{1,0:T(8,128)(2,1)S(1)}, bf16[256,1024]{1,0:T(8,128)(2,1)S(1)}, u32[]{:S(2)}, u32[]{:S(2)}) collective-permute-start(bf16[256,1024]{1,0:T(8,128)(2,1)S(1)} %dynamic-slice_bitcast_fusion), channel_id=1, source_target_pairs={{0,1},{1,0},{2,3},{3,2},{4,5},{5,4},{6,7},{7,6},{8,9},{9,8},{10,11... | collective-permute-start | bytes 1572872 | tf_op jit(solution)/shard_map/ppermute | solution.py:303
  262.4 50.4 %collective-permute-start.25 = (bf16[2,2,2,1,64,4608]{5,4,3,2,1,0:T(8,128)(2,1)}, bf16[2,2,2,1,64,4608]{5,4,3,2,1,0:T(8,128)(2,1)}, u32[]{:S(2)}, u32[]{:S(2)}) collective-permute-start(bf16[2,2,2,1,64,4608]{5,4,3,2,1,0:T(8,128)(2,1)} %pad_maximum_fusion.5), channel_id=1, source_target_pairs={{0,2},{2,0},{4,6},{6,4},{8,10},{10,8},{12,14},{14,12},{16,18},{18,... | collective-permute-start | bytes 14155784 | tf_op jit(solution)/shard_map/ppermute | solution.py:332
  380.2 54.8 %collective-permute-start.30 = (bf16[2,2,2,1,64,4608]{5,4,3,2,1,0:T(8,128)(2,1)}, bf16[2,2,2,1,64,4608]{5,4,3,2,1,0:T(8,128)(2,1)}, u32[]{:S(2)}, u32[]{:S(2)}) collective-permute-start(bf16[2,2,2,1,64,4608]{5,4,3,2,1,0:T(8,128)(2,1)} %split.155), channel_id=1, source_target_pairs={{0,2},{2,0},{4,6},{6,4},{8,10},{10,8},{12,14},{14,12},{16,18},{18,... | collective-permute-start | bytes 14155784 | tf_op jit(solution)/shard_map/ppermute | solution.py:332
  402.9 38.1 %collective-permute-start.29 = (bf16[2,2,2,1,64,4608]{5,4,3,2,1,0:T(8,128)(2,1)}, bf16[2,2,2,1,64,4608]{5,4,3,2,1,0:T(8,128)(2,1)}, u32[]{:S(2)}, u32[]{:S(2)}) collective-permute-start(bf16[2,2,2,1,64,4608]{5,4,3,2,1,0:T(8,128)(2,1)} %split.153), channel_id=1, source_target_pairs={{0,2},{2,0},{4,6},{6,4},{8,10},{10,8},{12,14},{14,12},{16,18},{18,... | collective-permute-start | bytes 14155784 | tf_op jit(solution)/shard_map/ppermute | solution.py:332
  408.1 40.2 %collective-permute-start.28 = (bf16[2,2,2,1,64,4608]{5,4,3,2,1,0:T(8,128)(2,1)}, bf16[2,2,2,1,64,4608]{5,4,3,2,1,0:T(8,128)(2,1)}, u32[]{:S(2)}, u32[]{:S(2)}) collective-permute-start(bf16[2,2,2,1,64,4608]{5,4,3,2,1,0:T(8,128)(2,1)} %split.151), channel_id=1, source_target_pairs={{0,2},{2,0},{4,6},{6,4},{8,10},{10,8},{12,14},{14,12},{16,18},{18,... | collective-permute-start | bytes 14155784 | tf_op jit(solution)/shard_map/ppermute | solution.py:332
  425.9 29.8 %collective-permute-start.26 = (bf16[256,1024]{1,0:T(8,128)(2,1)}, bf16[256,1024]{1,0:T(8,128)(2,1)}, u32[]{:S(2)}, u32[]{:S(2)}) collective-permute-start(bf16[256,1024]{1,0:T(8,128)(2,1)} %dynamic-slice_bitcast_fusion.1), channel_id=1, source_target_pairs={{0,1},{1,0},{2,3},{3,2},{4,5},{5,4},{6,7},{7,6},{8,9},{9,8},{10,11... | collective-permute-start | bytes 1572872 | tf_op jit(solution)/shard_map/ppermute | solution.py:303
  455.4 15.0 %collective-permute-start.48 = (bf16[2,2,2,1,64,1024]{5,4,3,2,1,0:T(8,128)(2,1)}, bf16[2,2,2,1,64,1024]{5,4,3,2,1,0:T(8,128)(2,1)}, u32[]{:S(2)}, u32[]{:S(2)}) collective-permute-start(bf16[2,2,2,1,64,1024]{5,4,3,2,1,0:T(8,128)(2,1)} %split.211), channel_id=1, source_target_pairs={{0,2},{2,0},{4,6},{6,4},{8,10},{10,8},{12,14},{14,12},{16,18},{18,... | collective-permute-start | bytes 3145736 | tf_op jit(solution)/shard_map/ppermute | solution.py:332
  462.0 58.7 %collective-permute-start.33 = (bf16[2,1,2,1,64,4608]{5,4,3,2,1,0:T(8,128)(2,1)}, bf16[2,1,2,1,64,4608]{5,4,3,2,1,0:T(8,128)(2,1)}, u32[]{:S(2)}, u32[]{:S(2)}) collective-permute-start(bf16[2,1,2,1,64,4608]{5,4,3,2,1,0:T(8,128)(2,1)} %split.161), channel_id=1, source_target_pairs={{0,8},{2,10},{4,12},{6,14},{8,0},{10,2},{12,4},{14,6},{16,24},{18,... | collective-permute-start | bytes 7077896 | tf_op jit(solution)/shard_map/ppermute | solution.py:332
  472.2 30.0 %collective-permute-start.49 = (bf16[2,2,1,1,64,1024]{5,4,3,2,1,0:T(8,128)(2,1)S(1)}, bf16[2,2,1,1,64,1024]{5,4,3,2,1,0:T(8,128)(2,1)S(1)}, u32[]{:S(2)}, u32[]{:S(2)}) collective-permute-start(bf16[2,2,1,1,64,1024]{5,4,3,2,1,0:T(8,128)(2,1)S(1)} %split.213), channel_id=1, source_target_pairs={{0,4},{2,6},{4,0},{6,2},{8,12},{10,14},{12,8},{14,10},{16,20},{18,... | collective-permute-start | bytes 1572872 | tf_op jit(solution)/shard_map/ppermute | solution.py:332
  501.4 53.2 %collective-permute-start.32 = (bf16[2,2,1,1,64,4608]{5,4,3,2,1,0:T(8,128)(2,1)}, bf16[2,2,1,1,64,4608]{5,4,3,2,1,0:T(8,128)(2,1)}, u32[]{:S(2)}, u32[]{:S(2)}) collective-permute-start(bf16[2,2,1,1,64,4608]{5,4,3,2,1,0:T(8,128)(2,1)} %split.159), channel_id=1, source_target_pairs={{0,4},{2,6},{4,0},{6,2},{8,12},{10,14},{12,8},{14,10},{16,20},{18,... | collective-permute-start | bytes 7077896 | tf_op jit(solution)/shard_map/ppermute | solution.py:332
  502.4 9.1 %collective-permute-start.50 = (bf16[2,2,1,1,64,512]{5,4,3,2,1,0:T(8,128)(2,1)S(1)}, bf16[2,2,1,1,64,512]{5,4,3,2,1,0:T(8,128)(2,1)S(1)}, u32[]{:S(2)}, u32[]{:S(2)}) collective-permute-start(bf16[2,2,1,1,64,512]{5,4,3,2,1,0:T(8,128)(2,1)S(1)} %split.215), channel_id=1, source_target_pairs={{0,1},{1,0},{2,3},{3,2},{4,5},{5,4},{6,7},{7,6},{8,9},{9,8},{10,11... | collective-permute-start | bytes 786440 | tf_op jit(solution)/shard_map/ppermute | solution.py:332
  511.6 7.5 collective-permute-start.51
  517.5 52.2 %collective-permute-start.31 = (bf16[2,2,2,1,64,2304]{5,4,3,2,1,0:T(8,128)(2,1)}, bf16[2,2,2,1,64,2304]{5,4,3,2,1,0:T(8,128)(2,1)}, u32[]{:S(2)}, u32[]{:S(2)}) collective-permute-start(bf16[2,2,2,1,64,2304]{5,4,3,2,1,0:T(8,128)(2,1)} %split.157), channel_id=1, source_target_pairs={{0,1},{1,0},{2,3},{3,2},{4,5},{5,4},{6,7},{7,6},{8,9},{9,8},{10,11... | collective-permute-start | bytes 7077896 | tf_op jit(solution)/shard_map/ppermute | solution.py:332
  519.8 164.7 %collective-permute-start.52 = (bf16[1,1,1,1,64,512]{5,4,3,2,1,0:T(8,128)(2,1)}, bf16[1,1,1,1,64,512]{5,4,3,2,1,0:T(8,128)(2,1)}, u32[]{:S(2)}, u32[]{:S(2)}) collective-permute-start(bf16[1,1,1,1,64,512]{5,4,3,2,1,0:T(8,128)(2,1)} %split.219), channel_id=1, source_target_pairs={{0,16},{2,18},{4,20},{6,22},{8,24},{10,26},{12,28},{14,30},{16,0},... | collective-permute-start | bytes 196616 | tf_op jit(solution)/shard_map/ppermute | solution.py:332
  520.7 53.3 %slice-start = ((s8[8388608]{0:T(1024)(128)(4,1)}), s8[4194304]{0:T(1024)(128)(4,1)S(1)}, s32[]{:S(2)}) async-start(s8[8388608]{0:T(1024)(128)(4,1)} %bitcast.196), calls=%async_computation | async-start | bytes 8388608
  599.7 51.6 %collective-permute-start.36 = (bf16[1,1,2,1,64,4608]{5,4,3,2,1,0:T(8,128)(2,1)S(1)}, bf16[1,1,2,1,64,4608]{5,4,3,2,1,0:T(8,128)(2,1)S(1)}, u32[]{:S(2)}, u32[]{:S(2)}) collective-permute-start(bf16[1,1,2,1,64,4608]{5,4,3,2,1,0:T(8,128)(2,1)S(1)} %split.167), channel_id=1, source_target_pairs={{0,16},{2,18},{4,20},{6,22},{8,24},{10,26},{12,28},{14,30},{16,0},... | collective-permute-start | bytes 3538952 | tf_op jit(solution)/shard_map/ppermute | solution.py:332
  600.8 25.5 %collective-permute-start.35 = (bf16[2,2,1,1,64,2304]{5,4,3,2,1,0:T(8,128)(2,1)S(1)}, bf16[2,2,1,1,64,2304]{5,4,3,2,1,0:T(8,128)(2,1)S(1)}, u32[]{:S(2)}, u32[]{:S(2)}) collective-permute-start(bf16[2,2,1,1,64,2304]{5,4,3,2,1,0:T(8,128)(2,1)S(1)} %split.165), channel_id=1, source_target_pairs={{0,1},{1,0},{2,3},{3,2},{4,5},{5,4},{6,7},{7,6},{8,9},{9,8},{10,11... | collective-permute-start | bytes 3538952 | tf_op jit(solution)/shard_map/ppermute | solution.py:332
  609.3 42.3 %collective-permute-start.34 = (bf16[2,2,1,1,64,2304]{5,4,3,2,1,0:T(8,128)(2,1)S(1)}, bf16[2,2,1,1,64,2304]{5,4,3,2,1,0:T(8,128)(2,1)S(1)}, u32[]{:S(2)}, u32[]{:S(2)}) collective-permute-start(bf16[2,2,1,1,64,2304]{5,4,3,2,1,0:T(8,128)(2,1)S(1)} %split.163), channel_id=1, source_target_pairs={{0,4},{2,6},{4,0},{6,2},{8,12},{10,14},{12,8},{14,10},{16,20},{18,... | collective-permute-start | bytes 3538952 | tf_op jit(solution)/shard_map/ppermute | solution.py:332
  661.5 42.1 %collective-permute-start.43 = (bf16[2,2,2,1,64,2048]{5,4,3,2,1,0:T(8,128)(2,1)}, bf16[2,2,2,1,64,2048]{5,4,3,2,1,0:T(8,128)(2,1)}, u32[]{:S(2)}, u32[]{:S(2)}) collective-permute-start(bf16[2,2,2,1,64,2048]{5,4,3,2,1,0:T(8,128)(2,1)} %split.201), channel_id=1, source_target_pairs={{0,2},{2,0},{4,6},{6,4},{8,10},{10,8},{12,14},{14,12},{16,18},{18,... | collective-permute-start | bytes 6291464 | tf_op jit(solution)/shard_map/ppermute | solution.py:332
  667.1 3.7 collective-permute-start.38
  670.9 4.8 collective-permute-start.39
  675.7 4.8 collective-permute-start.40
  680.5 4.0 collective-permute-start.41
  682.5 12.4 %collective-permute-start.37 = (bf16[256,1024]{1,0:T(8,128)(2,1)S(1)}, bf16[256,1024]{1,0:T(8,128)(2,1)S(1)}, u32[]{:S(2)}, u32[]{:S(2)}) collective-permute-start(bf16[256,1024]{1,0:T(8,128)(2,1)S(1)} %fusion.64), channel_id=1, source_target_pairs={{0,1},{1,0},{2,3},{3,2},{4,5},{5,4},{6,7},{7,6},{8,9},{9,8},{10,11... | collective-permute-start | bytes 1572872 | tf_op jit(solution)/shard_map/ppermute | solution.py:303
  684.5 4.9 collective-permute-start.42
  686.1 15.8 %collective-permute-start.57 = (bf16[1,1,1,1,64,4608]{5,4,3,2,1,0:T(8,128)(2,1)S(1)}, bf16[1,1,1,1,64,4608]{5,4,3,2,1,0:T(8,128)(2,1)S(1)}, u32[]{:S(2)}, u32[]{:S(2)}) collective-permute-start(bf16[1,1,1,1,64,4608]{5,4,3,2,1,0:T(8,128)(2,1)S(1)} %split.197), channel_id=1, source_target_pairs={{0,4},{2,6},{4,0},{6,2},{8,12},{10,14},{12,8},{14,10},{16,20},{18,... | collective-permute-start | bytes 1769480 | tf_op jit(solution)/shard_map/ppermute | solution.py:332
  687.8 18.9 %collective-permute-start.55 = (bf16[2,1,1,1,64,2304]{5,4,3,2,1,0:T(8,128)(2,1)S(1)}, bf16[2,1,1,1,64,2304]{5,4,3,2,1,0:T(8,128)(2,1)S(1)}, u32[]{:S(2)}, u32[]{:S(2)}) collective-permute-start(bf16[2,1,1,1,64,2304]{5,4,3,2,1,0:T(8,128)(2,1)S(1)} %split.193), channel_id=1, source_target_pairs={{0,8},{2,10},{4,12},{6,14},{8,0},{10,2},{12,4},{14,6},{16,24},{18,... | collective-permute-start | bytes 1769480 | tf_op jit(solution)/shard_map/ppermute | solution.py:332
  689.4 32.9 %collective-permute-start.53 = (bf16[2,1,1,1,64,2304]{5,4,3,2,1,0:T(8,128)(2,1)S(1)}, bf16[2,1,1,1,64,2304]{5,4,3,2,1,0:T(8,128)(2,1)S(1)}, u32[]{:S(2)}, u32[]{:S(2)}) collective-permute-start(bf16[2,1,1,1,64,2304]{5,4,3,2,1,0:T(8,128)(2,1)S(1)} %split.189), channel_id=1, source_target_pairs={{0,8},{2,10},{4,12},{6,14},{8,0},{10,2},{12,4},{14,6},{16,24},{18,... | collective-permute-start | bytes 1769480 | tf_op jit(solution)/shard_map/ppermute | solution.py:332
  702.1 33.2 %collective-permute-start.58 = (bf16[1,1,1,1,64,2304]{5,4,3,2,1,0:T(8,128)(2,1)S(1)}, bf16[1,1,1,1,64,2304]{5,4,3,2,1,0:T(8,128)(2,1)S(1)}, u32[]{:S(2)}, u32[]{:S(2)}) collective-permute-start(bf16[1,1,1,1,64,2304]{5,4,3,2,1,0:T(8,128)(2,1)S(1)} %split.225), channel_id=1, source_target_pairs={{0,1},{1,0},{2,3},{3,2},{4,5},{5,4},{6,7},{7,6},{8,9},{9,8},{10,11... | collective-permute-start | bytes 884744 | tf_op jit(solution)/shard_map/ppermute | solution.py:332
  706.1 27.1 %collective-permute-start.44 = (bf16[2,2,2,1,64,1024]{5,4,3,2,1,0:T(8,128)(2,1)S(1)}, bf16[2,2,2,1,64,1024]{5,4,3,2,1,0:T(8,128)(2,1)S(1)}, u32[]{:S(2)}, u32[]{:S(2)}) collective-permute-start(bf16[2,2,2,1,64,1024]{5,4,3,2,1,0:T(8,128)(2,1)S(1)} %split.203), channel_id=1, source_target_pairs={{0,1},{1,0},{2,3},{3,2},{4,5},{5,4},{6,7},{7,6},{8,9},{9,8},{10,11... | collective-permute-start | bytes 3145736 | tf_op jit(solution)/shard_map/ppermute | solution.py:332
  706.9 41.3 %collective-permute-start.56 = (bf16[1,1,1,1,64,2304]{5,4,3,2,1,0:T(8,128)(2,1)S(1)}, bf16[1,1,1,1,64,2304]{5,4,3,2,1,0:T(8,128)(2,1)S(1)}, u32[]{:S(2)}, u32[]{:S(2)}) collective-permute-start(bf16[1,1,1,1,64,2304]{5,4,3,2,1,0:T(8,128)(2,1)S(1)} %split.223), channel_id=1, source_target_pairs={{0,16},{2,18},{4,20},{6,22},{8,24},{10,26},{12,28},{14,30},{16,0},... | collective-permute-start | bytes 884744 | tf_op jit(solution)/shard_map/ppermute | solution.py:332
  722.4 32.6 %collective-permute-start.54 = (bf16[1,1,1,1,64,2304]{5,4,3,2,1,0:T(8,128)(2,1)S(1)}, bf16[1,1,1,1,64,2304]{5,4,3,2,1,0:T(8,128)(2,1)S(1)}, u32[]{:S(2)}, u32[]{:S(2)}) collective-permute-start(bf16[1,1,1,1,64,2304]{5,4,3,2,1,0:T(8,128)(2,1)S(1)} %split.221), channel_id=1, source_target_pairs={{0,16},{2,18},{4,20},{6,22},{8,24},{10,26},{12,28},{14,30},{16,0},... | collective-permute-start | bytes 884744 | tf_op jit(solution)/shard_map/ppermute | solution.py:332
  733.7 12.7 %collective-permute-start.45 = (bf16[2,2,1,1,64,1024]{5,4,3,2,1,0:T(8,128)(2,1)S(1)}, bf16[2,2,1,1,64,1024]{5,4,3,2,1,0:T(8,128)(2,1)S(1)}, u32[]{:S(2)}, u32[]{:S(2)}) collective-permute-start(bf16[2,2,1,1,64,1024]{5,4,3,2,1,0:T(8,128)(2,1)S(1)} %split.205), channel_id=1, source_target_pairs={{0,4},{2,6},{4,0},{6,2},{8,12},{10,14},{12,8},{14,10},{16,20},{18,... | collective-permute-start | bytes 1572872 | tf_op jit(solution)/shard_map/ppermute | solution.py:332
  746.6 6.4 collective-permute-start.46
  753.2 7.3 collective-permute-start.47
  (108 other events, 919.4 us)
